TPU v7x, 128 devices: a whole 4x4x4 slice. The times are simulated.
128 devices in a mesh: row: 16 (over x_hi, y, core), col: 8 (over x_lo, z).
Axes of the slice: x: 4 (x_hi: 2, x_lo: 2; x = x_hi * 2 + x_lo), y: 4, z: 4, core: 2. Of those that a mesh axis runs over, the one named last changes fastest.
Arguments:
- vectors: float32 [131072, 2048], P('row', 'col'), may hold values from -6 to 6
- reflectors: float32 [131072, 512], P('row', 'col'), may hold values from -0.046875 to 0.046875
- tmat: float32 [512, 512], replicated, as said below
- offset: int32 [1], replicated, may hold values from 0 to 32767
- band: int32 [1], replicated, may hold values from 65536 to 98303
Outputs:
- updated: float32 [131072, 2048], P('row', 'col')
Inputs may be any that keep to these rules, and one draw needn't show every extreme that they name: tmat is upper triangular with a positive diagonal.
All inputs are finite; a program needn't handle non-finite values.
Results may differ from a plain program's by a relative error of at most 0.000092.
Values sent between devices are 32-bit elements; how exact they have to be, the bound alone decides.
No kernel may reach another device: no remote copies, remote signals or barrier semaphores. Data moves between devices by JAX's collectives and lax.ppermute only.
A program may use at most 128 MiB of HBM per device.

v0:
```python
import functools

import jax
import jax.numpy as jnp
from jax import lax
from jax.experimental import pallas as pl
from jax.experimental.pallas import tpu as pltpu
from jax.sharding import PartitionSpec as P

TILE = 64
BLOCK = 2 * TILE
WINDOW = 50
SPAN = WINDOW * BLOCK
STEP = 10
ORDER = (0, 1, 3, 2)
CHUNKS = 2
ROWS = 16
F32, BF16 = jnp.float32, jnp.bfloat16


def col_perm(dl, dz):
    return [
        (low * 4 + z, (low ^ dl) * 4 + (z + dz) % 4) for low in range(2) for z in range(4)
    ]


def tile_kernel(y_ref, *out_refs):
    lanes = lax.broadcasted_iota(jnp.int32, (y_ref.shape[0], BLOCK), 1)
    low = lanes < TILE
    rows = y_ref.shape[0] // CHUNKS
    for q in range(8):
        first = y_ref[:, q * BLOCK : (q + 1) * BLOCK]
        second = y_ref[:, 1024 + q * BLOCK : 1024 + (q + 1) * BLOCK]
        even = jnp.where(low, first, pltpu.roll(second, TILE, 1))
        odd = jnp.where(low, pltpu.roll(first, TILE, 1), second)
        for k, out in enumerate(out_refs):
            out[2 * q, 0] = even[k * rows : (k + 1) * rows]
            out[2 * q + 1, 0] = odd[k * rows : (k + 1) * rows]


def cut_tiles(y_t):
    refl, height = y_t.shape
    steps = height // 2048
    rows = refl // CHUNKS
    return pl.pallas_call(
        tile_kernel,
        grid=(steps,),
        in_specs=[pl.BlockSpec((refl, 2048), lambda i: (0, i))],
        out_specs=[pl.BlockSpec((ROWS, 1, rows, BLOCK), lambda i: (0, i, 0, 0))] * CHUNKS,
        out_shape=[jax.ShapeDtypeStruct((ROWS, steps, rows, BLOCK), F32)] * CHUNKS,
        name="cut_tiles",
    )(y_t)


def split(value):
    high = value.astype(BF16)
    return high, (value - high.astype(F32)).astype(BF16)


def window_rows(width, lane=0):
    return pl.BlockSpec(
        (pl.Element(STEP * BLOCK), pl.Element(width)),
        lambda i, s: (pl.multiple_of((s[0] + i * STEP) * BLOCK, BLOCK), lane),
    )


def prepare_kernel(info, *refs):
    chunk_refs, (high, low, high_t, low_t) = refs[: 2 * CHUNKS], refs[-4:]
    rows = chunk_refs[0].shape[2]
    step = pl.program_id(0)
    lane = lax.broadcasted_iota(jnp.int32, (rows, BLOCK), 1)
    spread = (lane // TILE) * (ROWS * TILE) + lane % TILE
    spread = spread - lax.broadcasted_iota(jnp.int32, (rows, BLOCK), 0)
    band = info[3]
    for w in range(STEP):
        start = (info[0] + step * STEP + w) * (BLOCK * ROWS) + info[1] * TILE - info[2]
        parts = []
        for half in range(2):
            for k in range(CHUNKS):
                raw = chunk_refs[2 * k + half][0, w]
                away = spread + (start - info[4 + half] - k * rows)
                kept = jnp.where((away > 0) & (away < band), raw, 0.0)
                parts.append(jnp.where(away == 0, 1.0, kept))
        value = jnp.concatenate(parts, axis=0)
        at = slice(w * BLOCK, (w + 1) * BLOCK)
        high[:, at], low[:, at] = split(value)
        high_t[at, :], low_t[at, :] = split(value.T)


def prepare(info, chunks, place, height, count, before):
    specs, arrays = [], []
    for halves in chunks:
        for array, lead in halves:
            rows = array.shape[2]
            specs.append(
                pl.BlockSpec((1, STEP, rows, BLOCK), functools.partial(lambda lead, i, s: (lead, i, 0, 0), lead))
            )
            arrays.append(array)
    aliases = {1 + len(arrays) + k: k for k in range(len(before))}
    specs += [pl.BlockSpec(memory_space=pl.ANY)] * len(before)
    wide = jax.ShapeDtypeStruct((count, SPAN), BF16)
    tall = jax.ShapeDtypeStruct((height, count), BF16)
    wide_spec = pl.BlockSpec((BLOCK, STEP * BLOCK), lambda i, s: (place, i))
    tall_spec = window_rows(BLOCK, place * BLOCK)
    return pl.pallas_call(
        prepare_kernel,
        grid_spec=pltpu.PrefetchScalarGridSpec(
            num_scalar_prefetch=1,
            grid=(WINDOW // STEP,),
            in_specs=specs,
            out_specs=[wide_spec, wide_spec, tall_spec, tall_spec],
        ),
        out_shape=[wide, wide, tall, tall],
        input_output_aliases=aliases,
        name="prepare",
        cost_estimate=pl.CostEstimate(flops=10**9, bytes_accessed=2 * 10**7, transcendentals=0),
    )(info, *arrays, *before)


def dot(a, b):
    return jnp.dot(a, b, preferred_element_type=F32)


def project_kernel(info, v_ref, high_ref, low_ref, out):
    @pl.when(pl.program_id(0) == 0)
    def _():
        out[...] = jnp.zeros_like(out)

    v_high, v_low = split(v_ref[...])
    high = high_ref[...]
    out[...] += dot(high, v_high) + dot(low_ref[...], v_high) + dot(high, v_low)


def project(info, cyc_v, high, low, start, count):
    width = cyc_v.shape[1]
    wide = pl.BlockSpec((count, STEP * BLOCK), lambda i, s: (start // count, i))
    return pl.pallas_call(
        project_kernel,
        grid_spec=pltpu.PrefetchScalarGridSpec(
            num_scalar_prefetch=1,
            grid=(WINDOW // STEP,),
            in_specs=[window_rows(width), wide, wide],
            out_specs=pl.BlockSpec((count, width), lambda i, s: (0, 0)),
        ),
        out_shape=jax.ShapeDtypeStruct((count, width), F32),
        name="project",
        cost_estimate=pl.CostEstimate(flops=6 * count * SPAN * 256, bytes_accessed=2 * 10**7, transcendentals=0),
    )(info, cyc_v, high, low)


def apply_kernel(info, v_ref, t_ref, p_ref, high_ref, low_ref, out, w_high, w_low):
    step = pl.program_id(0)
    rows = v_ref.shape[0]

    @pl.when(step == 0)
    def _():
        t_high, t_low = split(t_ref[...])
        p_high, p_low = split(p_ref[...])
        weights = dot(t_high, p_high) + dot(t_low, p_high) + dot(t_high, p_low)
        w_high[...], w_low[...] = split(weights)

    start = info[0] * BLOCK - step * rows
    touched = (start < rows) & (start + SPAN > 0)

    @pl.when(touched)
    def _():
        high = high_ref[...]
        change = dot(high, w_high[...]) + dot(low_ref[...], w_high[...]) + dot(high, w_low[...])
        at = lax.broadcasted_iota(jnp.int32, change.shape, 0) - start
        value = v_ref[...]
        out[...] = jnp.where((at >= 0) & (at < SPAN), value - change, value)

    @pl.when(jnp.logical_not(touched))
    def _():
        out[...] = v_ref[...]


def apply(info, cyc_v, t_rel, products, high, low):
    nb, (height, width) = high.shape[1], cyc_v.shape
    rows = 8 * BLOCK
    tall = pl.BlockSpec((rows, nb), lambda i, s: (i, 0))
    plain = pl.BlockSpec((rows, width), lambda i, s: (i, 0))
    return pl.pallas_call(
        apply_kernel,
        grid_spec=pltpu.PrefetchScalarGridSpec(
            num_scalar_prefetch=1,
            grid=(height // rows,),
            in_specs=[
                plain,
                pl.BlockSpec((nb, nb), lambda i, s: (0, 0)),
                pl.BlockSpec((nb, width), lambda i, s: (0, 0)),
            ]
            + [tall] * 2,
            out_specs=plain,
            scratch_shapes=[pltpu.VMEM((nb, width), BF16)] * 2,
        ),
        out_shape=jax.ShapeDtypeStruct(cyc_v.shape, F32),
        name="apply",
        cost_estimate=pl.CostEstimate(flops=6 * 512 * SPAN * 256, bytes_accessed=3 * 10**7, transcendentals=0),
    )(info, cyc_v, t_rel, products, high, low)


def per_device(vectors, reflectors, tmat, offset, band):
    height, width = vectors.shape
    refl = reflectors.shape[1]
    nb = 8 * refl
    position = lax.axis_index("row")
    place = lax.axis_index("col")
    xl, zz = place // 4, place % 4
    w0 = jnp.clip(offset[0] // (BLOCK * ROWS), 0, height // BLOCK - WINDOW)

    pieces = [
        lax.all_to_all(piece, "row", split_axis=0, concat_axis=0, tiled=True)
        for piece in cut_tiles(reflectors.T)
    ]
    pairs = []
    for piece in pieces:
        rows = piece.shape[2]
        cyc = piece.reshape(height // BLOCK, rows, BLOCK)
        mine = lax.dynamic_slice_in_dim(cyc, w0, WINDOW, 0)
        across = lax.ppermute(mine, "col", col_perm(1, 0))
        pairs.append(jnp.stack([mine, across]))

    source = vectors.reshape(height // (ROWS * TILE), ROWS, TILE, width).transpose(1, 0, 2, 3)
    source, *_ = lax.optimization_barrier((source, *pairs))
    cyc_v = lax.all_to_all(source, "row", split_axis=0, concat_axis=0, tiled=True).reshape(height, width)

    groups = [[], [], [], []]
    for pair in pairs:
        up = lax.ppermute(pair, "col", col_perm(0, 1))
        down = lax.ppermute(pair, "col", col_perm(0, 3))
        far0 = lax.ppermute(up[:1], "col", col_perm(0, 1))
        far1 = lax.ppermute(down[1:], "col", col_perm(0, 3))
        groups[0].append(((pair, 0), (pair, 1)))
        groups[1].append(((down, 0), (down, 1)))
        groups[2].append(((far0, 0), (far1, 0)))
        groups[3].append(((up, 0), (up, 1)))

    ready = ()
    ids = []
    for n, g in enumerate(ORDER):
        base = ((zz + g) % 4) * refl
        starts = [(xl ^ half) * 4 * refl + base for half in range(2)]
        info = jnp.stack([w0, position, offset[0], band[0], *starts]).astype(jnp.int32)
        ready = prepare(info, groups[g], n, height, nb, ready)
        ids += [start + jnp.arange(refl) for start in starts]
    ids = jnp.concatenate(ids)
    high, low, high_t, low_t = ready

    info = w0[None].astype(jnp.int32)
    partial_value = project(info, cyc_v, high, low, 0, nb)
    share = lax.all_to_all(
        partial_value.reshape(ROWS, nb // ROWS, width), "row", split_axis=0, concat_axis=0, tiled=True
    ).sum(0)
    products = lax.all_to_all(
        jnp.broadcast_to(share[None], (ROWS, nb // ROWS, width)),
        "row", split_axis=0, concat_axis=0, tiled=True,
    ).reshape(nb, width)
    t_rel = tmat[ids][:, ids]
    return apply(info, cyc_v, t_rel, products, high_t, low_t)


def solution(mesh):
    placed = (P("row", "col"), P("row", "col"), P(), P(), P())
    return jax.shard_map(
        per_device, mesh=mesh, in_specs=placed, out_specs=P("row", "col"), check_vma=False
    )
```

profile of v0, /device:TPU:1, one launch (start us, length us, event | category | flops | bytes accessed | tf_op | source)
XLA Modules:
  0.0 281.8 jit_solution(5701204861708870599)
XLA Ops:
  0.0 4.2 %cut_tiles.1 = (f32[16,4,32,128]{3,2,1,0:T(8,128)}, f32[16,4,32,128]{3,2,1,0:T(8,128)}) custom-call(f32[64,8192]{1,0:T(8,128)} %bitcast.57), custom_call_target="tpu_custom_call" | custom-call | tf_op jit(solution)/shard_map/cut_tiles/pallas_call | solution.py:45
  4.2 25.4 %all_to_all.25 = f32[16,4,32,128]{3,2,1,0:T(8,128)S(1)} all-to-all(f32[16,4,32,128]{3,2,1,0:T(8,128)} %get-tuple-element.24), channel_id=1, replica_groups=mesh['row'=16,'col'=8] {'row'}, dimensions={0} | all-to-all | bytes 2097152 | tf_op jit(solution)/shard_map/all_to_all | solution.py:213
  29.6 4.6 %all-to-all-start.1 = ((f32[16,4,32,128]{3,2,1,0:T(8,128)}), f32[16,4,32,128]{3,2,1,0:T(8,128)S(1)}, u32[]{:S(2)}, u32[]{:S(2)}) async-start(f32[16,4,32,128]{3,2,1,0:T(8,128)} %get-tuple-element.25), calls=%async_computation.1 | async-start | bytes 2097152 | tf_op jit(solution)/shard_map/all_to_all | solution.py:213
  36.2 15.3 %all-to-all-done.1 = f32[16,4,32,128]{3,2,1,0:T(8,128)S(1)} async-done(((f32[16,4,32,128]{3,2,1,0:T(8,128)}), f32[16,4,32,128]{3,2,1,0:T(8,128)S(1)}, u32[]{:S(2)}, u32[]{:S(2)}) %all-to-all-start.1) | async-done | bytes 1048608 | tf_op jit(solution)/shard_map/all_to_all | solution.py:213
  52.0 7.9 %copy.22 = f32[8,16,64,256]{3,2,0,1:T(8,128)} copy(f32[8,16,64,256]{3,2,1,0:T(8,128)} %bitcast.50) | data formatting | bytes 16777216 | tf_op jit(solution)/shard_map/reshape | solution.py:224
  60.0 4.6 %collective-permute-done = f32[50,32,128]{2,1,0:T(8,128)} collective-permute-done((f32[50,32,128]{2,1,0:T(8,128)}, f32[50,32,128]{2,1,0:T(8,128)}, u32[]{:S(2)}, u32[]{:S(2)}) %collective-permute-start) | collective-permute-done | bytes 819232 | tf_op jit(solution)/shard_map/ppermute | solution.py:221
  65.9 16.1 %collective-permute-done.1 = f32[50,32,128]{2,1,0:T(8,128)S(1)} collective-permute-done((f32[50,32,128]{2,1,0:T(8,128)S(1)}, f32[50,32,128]{2,1,0:T(8,128)S(1)}, u32[]{:S(2)}, u32[]{:S(2)}) %collective-permute-start.1) | collective-permute-done | bytes 819232 | tf_op jit(solution)/shard_map/ppermute | solution.py:221
  83.3 8.2 %all-to-all-start.2 = ((f32[16,8,64,256]{3,2,1,0:T(8,128)}), f32[16,8,64,256]{3,2,1,0:T(8,128)}, u32[]{:S(2)}, u32[]{:S(2)}) async-start(f32[16,8,64,256]{3,2,1,0:T(8,128)} %bitcast.49), calls=%async_computation.2 | async-start | bytes 16777216 | tf_op jit(solution)/shard_map/all_to_all | solution.py:226
  93.1 2.2 collective-permute-start.4
  95.3 2.7 collective-permute-start.8
  98.0 33.4 %collective-permute-done.2.refs_0_.refs_1_ = f32[2,50,32,128]{3,2,1,0:T(8,128)S(1)} collective-permute-done((f32[2,50,32,128]{3,2,1,0:T(8,128)S(1)}, f32[2,50,32,128]{3,2,1,0:T(8,128)S(1)}, u32[]{:S(2)}, u32[]{:S(2)}) %collective-permute-start.2) | collective-permute-done | bytes 1638432 | tf_op jit(solution)/shard_map/ppermute | solution.py:230
  134.3 32.2 %collective-permute-done.6.refs_2_.refs_3_ = f32[2,50,32,128]{3,2,1,0:T(8,128)S(1)} collective-permute-done((f32[2,50,32,128]{3,2,1,0:T(8,128)}, f32[2,50,32,128]{3,2,1,0:T(8,128)S(1)}, u32[]{:S(2)}, u32[]{:S(2)}) %collective-permute-start.6) | collective-permute-done | bytes 1638432 | tf_op jit(solution)/shard_map/ppermute | solution.py:230
  170.0 2.7 collective-permute-start.9
  175.9 8.0 %prepare.4 = (bf16[512,6400]{1,0:T(8,128)(2,1)}, bf16[512,6400]{1,0:T(8,128)(2,1)}, bf16[8192,512]{1,0:T(8,128)(2,1)}, bf16[8192,512]{1,0:T(8,128)(2,1)}) custom-call(s32[6]{0:T(128)} %stack.82.info, f32[2,50,32,128]{3,2,1,0:T(8,128)} %copy-done.1, f32[2,50,32,128]{3,2,1,0:T(8,128)} %copy-done.1, f32[2,50,32,128]{3,2,1,0:T(8,128)} %pad_maximum_fusion.1.refs_2_.refs_3_, ...), custom_call_target="tpu_custom_call" | custom-call | flops 1000000000 | bytes 20000000 | tf_op jit(solution)/shard_map/prepare/pallas_call | solution.py:105
  183.9 7.9 %prepare.5 = (bf16[512,6400]{1,0:T(8,128)(2,1)}, bf16[512,6400]{1,0:T(8,128)(2,1)}, bf16[8192,512]{1,0:T(8,128)(2,1)}, bf16[8192,512]{1,0:T(8,128)(2,1)}) custom-call(s32[6]{0:T(128)} %stack.79.info, f32[2,50,32,128]{3,2,1,0:T(8,128)} %copy-done.4, ...), custom_call_target="tpu_custom_call", output_to_operand_aliasing={{0}: (5, {}), {1}: (6, {}), {2}: (7, {}), {3}: (8, {})} | custom-call | flops 1000000000 | bytes 20000000 | tf_op jit(solution)/shard_map/prepare/pallas_call | solution.py:105
  191.8 7.9 %prepare.6 = (bf16[512,6400]{1,0:T(8,128)(2,1)}, bf16[512,6400]{1,0:T(8,128)(2,1)}, bf16[8192,512]{1,0:T(8,128)(2,1)}, bf16[8192,512]{1,0:T(8,128)(2,1)}) custom-call(s32[6]{0:T(128)} %stack.76.info, f32[2,50,32,128]{3,2,1,0:T(8,128)} %copy-done.2, ...), custom_call_target="tpu_custom_call", output_to_operand_aliasing={{0}: (5, {}), {1}: (6, {}), {2}: (7, {}), {3}: (8, {})} | custom-call | flops 1000000000 | bytes 20000000 | tf_op jit(solution)/shard_map/prepare/pallas_call | solution.py:105
  199.8 1.9 collective-permute-done.7.refs_2_
  201.6 8.0 %prepare.7 = (bf16[512,6400]{1,0:T(8,128)(2,1)}, bf16[512,6400]{1,0:T(8,128)(2,1)}, bf16[8192,512]{1,0:T(8,128)(2,1)}, bf16[8192,512]{1,0:T(8,128)(2,1)}) custom-call(s32[6]{0:T(128)} %stack.73.info, f32[1,50,32,128]{3,2,1,0:T(8,128)} %collective-permute-done.3.refs_0_, ...), custom_call_target="tpu_custom_call", output_to_operand_aliasing={{0}: (5, {}), {1}: (6, {}), {2}: (7, {}), {3}: (8, {})} | custom-call | flops 1000000000 | bytes 20000000 | tf_op jit(solution)/shard_map/prepare/pallas_call | solution.py:105
  210.9 10.8 %project.1 = f32[512,256]{1,0:T(8,128)} custom-call(s32[1]{0:T(128)} %bitcast.1.info, f32[8192,256]{1,0:T(8,128)} %bitcast.11.v_ref, bf16[512,6400]{1,0:T(8,128)(2,1)} %get-tuple-element.39.high_ref, bf16[512,6400]{1,0:T(8,128)(2,1)} %get-tuple-element.40.low_ref), custom_call_target="tpu_custom_call" | custom-call | flops 5033164800 | bytes 20000000 | tf_op jit(solution)/shard_map/project/pallas_call | solution.py:137
  221.7 14.9 %all-to-all-start.3 = ((f32[16,32,256]{2,1,0:T(8,128)}), f32[16,32,256]{2,1,0:T(8,128)S(1)}, u32[]{:S(2)}, u32[]{:S(2)}) async-start(f32[16,32,256]{2,1,0:T(8,128)} %bitcast.56), calls=%async_computation.3 | async-start | bytes 1048576 | tf_op jit(solution)/shard_map/all_to_all | solution.py:252
  236.6 11.3 %all-to-all-done.3 = f32[16,32,256]{2,1,0:T(8,128)S(1)} async-done(((f32[16,32,256]{2,1,0:T(8,128)}), f32[16,32,256]{2,1,0:T(8,128)S(1)}, u32[]{:S(2)}, u32[]{:S(2)}) %all-to-all-start.3) | async-done | bytes 524320 | tf_op jit(solution)/shard_map/all_to_all | solution.py:252
  248.8 5.1 %all-to-all-start.4 = ((f32[16,32,256]{2,1,0:T(8,128)}), f32[16,32,256]{2,1,0:T(8,128)}, u32[]{:S(2)}, u32[]{:S(2)}) async-start(f32[16,32,256]{2,1,0:T(8,128)} %broadcast_in_dim.5), calls=%async_computation.4 | async-start | bytes 1048576 | tf_op jit(solution)/shard_map/all_to_all | solution.py:255
  259.0 6.4 %all-to-all-done.4 = f32[16,32,256]{2,1,0:T(8,128)} async-done(((f32[16,32,256]{2,1,0:T(8,128)}), f32[16,32,256]{2,1,0:T(8,128)}, u32[]{:S(2)}, u32[]{:S(2)}) %all-to-all-start.4) | async-done | bytes 524320 | tf_op jit(solution)/shard_map/all_to_all | solution.py:255
  265.4 16.4 %apply.1 = f32[8192,256]{1,0:T(8,128)} custom-call(s32[1]{0:T(128)} %bitcast.1.info, f32[8192,256]{1,0:T(8,128)} %bitcast.11.v_ref, f32[512,512]{1,0:T(8,128)} %bitcast.55, f32[512,256]{1,0:T(8,128)} %bitcast.32.p_ref, bf16[8192,512]{1,0:T(8,128)(2,1)} %get-tuple-element.41.high_ref, bf16[8192,512]{1,0:T(8,128)(2,1)} %get-tuple-element.42.low_ref), custom_call_target="tpu_custom_call" | custom-call | flops 5033164800 | bytes 30000000 | tf_op jit(solution)/shard_map/apply/pallas_call | solution.py:183
  (52 shorter events, 22.4 us)
Async XLA Ops:
  0.0 254.0 %copy-start = (f32[512,512]{1,0:T(8,128)S(1)}, f32[512,512]{1,0:T(8,128)}, u32[]{:S(2)}) copy-start(f32[512,512]{1,0:T(8,128)} %param.7) | copy-start | bytes 3145732
  29.6 21.9 %all-to-all-start.1 = ((f32[16,4,32,128]{3,2,1,0:T(8,128)}), f32[16,4,32,128]{3,2,1,0:T(8,128)S(1)}, u32[]{:S(2)}, u32[]{:S(2)}) async-start(f32[16,4,32,128]{3,2,1,0:T(8,128)} %get-tuple-element.25), calls=%async_computation.1 | async-start | bytes 2097152 | tf_op jit(solution)/shard_map/all_to_all | solution.py:213
  35.8 28.7 %collective-permute-start = (f32[50,32,128]{2,1,0:T(8,128)}, f32[50,32,128]{2,1,0:T(8,128)}, u32[]{:S(2)}, u32[]{:S(2)}) collective-permute-start(f32[50,32,128]{2,1,0:T(8,128)} %constant_dynamic-slice_fusion.1), channel_id=1, source_target_pairs={{0,4},{1,5},{2,6},{3,7},{4,0},{5,1},{6,2},{7,3},{8,12},{9,13},{10,... | collective-permute-start | bytes 2457608 | tf_op jit(solution)/shard_map/ppermute | solution.py:221
  51.5 30.5 %collective-permute-start.1 = (f32[50,32,128]{2,1,0:T(8,128)S(1)}, f32[50,32,128]{2,1,0:T(8,128)S(1)}, u32[]{:S(2)}, u32[]{:S(2)}) collective-permute-start(f32[50,32,128]{2,1,0:T(8,128)S(1)} %constant_dynamic-slice_fusion), channel_id=1, source_target_pairs={{0,4},{1,5},{2,6},{3,7},{4,0},{5,1},{6,2},{7,3},{8,12},{9,13},{10,... | collective-permute-start | bytes 2457608 | tf_op jit(solution)/shard_map/ppermute | solution.py:221
  65.9 27.2 %copy-start.1 = (f32[2,50,32,128]{3,2,1,0:T(8,128)}, f32[2,50,32,128]{3,2,1,0:T(8,128)S(1)}, u32[]{:S(2)}) copy-start(f32[2,50,32,128]{3,2,1,0:T(8,128)S(1)} %pad_maximum_fusion.refs_0_.refs_1_) | copy-start | bytes 4915204
  83.3 127.6 %all-to-all-start.2 = ((f32[16,8,64,256]{3,2,1,0:T(8,128)}), f32[16,8,64,256]{3,2,1,0:T(8,128)}, u32[]{:S(2)}, u32[]{:S(2)}) async-start(f32[16,8,64,256]{3,2,1,0:T(8,128)} %bitcast.49), calls=%async_computation.2 | async-start | bytes 16777216 | tf_op jit(solution)/shard_map/all_to_all | solution.py:226
  91.5 39.9 %collective-permute-start.2 = (f32[2,50,32,128]{3,2,1,0:T(8,128)S(1)}, f32[2,50,32,128]{3,2,1,0:T(8,128)S(1)}, u32[]{:S(2)}, u32[]{:S(2)}) collective-permute-start(f32[2,50,32,128]{3,2,1,0:T(8,128)S(1)} %pad_maximum_fusion.refs_0_.refs_1_), channel_id=1, source_target_pairs={{0,1},{1,2},{2,3},{3,0},{4,5},{5,6},{6,7},{7,4},{8,9},{9,10},{10,1... | collective-permute-start | bytes 4915208 | tf_op jit(solution)/shard_map/ppermute | solution.py:230
  93.1 38.4 %collective-permute-start.4 = (f32[2,50,32,128]{3,2,1,0:T(8,128)S(1)}, f32[2,50,32,128]{3,2,1,0:T(8,128)S(1)}, u32[]{:S(2)}, u32[]{:S(2)}) collective-permute-start(f32[2,50,32,128]{3,2,1,0:T(8,128)S(1)} %pad_maximum_fusion.refs_0_.refs_1_), channel_id=1, source_target_pairs={{0,3},{1,0},{2,1},{3,2},{4,7},{5,4},{6,5},{7,6},{8,11},{9,8},{10,9... | collective-permute-start | bytes 4915208 | tf_op jit(solution)/shard_map/ppermute | solution.py:231
  95.3 71.2 %collective-permute-start.6 = (f32[2,50,32,128]{3,2,1,0:T(8,128)}, f32[2,50,32,128]{3,2,1,0:T(8,128)S(1)}, u32[]{:S(2)}, u32[]{:S(2)}) collective-permute-start(f32[2,50,32,128]{3,2,1,0:T(8,128)} %pad_maximum_fusion.1.refs_2_.refs_3_), channel_id=1, source_target_pairs={{0,1},{1,2},{2,3},{3,0},{4,5},{5,6},{6,7},{7,4},{8,9},{9,10},{10,1... | collective-permute-start | bytes 4915208 | tf_op jit(solution)/shard_map/ppermute | solution.py:230
  95.3 72.5 %collective-permute-start.8 = (f32[2,50,32,128]{3,2,1,0:T(8,128)}, f32[2,50,32,128]{3,2,1,0:T(8,128)S(1)}, u32[]{:S(2)}, u32[]{:S(2)}) collective-permute-start(f32[2,50,32,128]{3,2,1,0:T(8,128)} %pad_maximum_fusion.1.refs_2_.refs_3_), channel_id=1, source_target_pairs={{0,3},{1,0},{2,1},{3,2},{4,7},{5,4},{6,5},{7,6},{8,11},{9,8},{10,9... | collective-permute-start | bytes 4915208 | tf_op jit(solution)/shard_map/ppermute | solution.py:231
  131.4 1.2 copy-start.2
  131.5 68.3 %collective-permute-start.3 = (f32[1,50,32,128]{3,2,1,0:T(8,128)S(1)}, f32[1,50,32,128]{3,2,1,0:T(8,128)}, u32[]{:S(2)}, u32[]{:S(2)}) collective-permute-start(f32[1,50,32,128]{3,2,1,0:T(8,128)S(1)} %slice.20), channel_id=1, source_target_pairs={{0,1},{1,2},{2,3},{3,0},{4,5},{5,6},{6,7},{7,4},{8,9},{9,10},{10,1... | collective-permute-start | bytes 2457608 | tf_op jit(solution)/shard_map/ppermute | solution.py:232
  132.6 35.2 %copy-start.4 = (f32[2,50,32,128]{3,2,1,0:T(8,128)}, f32[2,50,32,128]{3,2,1,0:T(8,128)S(1)}, u32[]{:S(2)}) copy-start(f32[2,50,32,128]{3,2,1,0:T(8,128)S(1)} %collective-permute-done.4.refs_0_.refs_1_) | copy-start | bytes 4915204
  132.6 67.1 %collective-permute-start.5 = (f32[1,50,32,128]{3,2,1,0:T(8,128)S(1)}, f32[1,50,32,128]{3,2,1,0:T(8,128)}, u32[]{:S(2)}, u32[]{:S(2)}) collective-permute-start(f32[1,50,32,128]{3,2,1,0:T(8,128)S(1)} %slice.21), channel_id=1, source_target_pairs={{0,3},{1,0},{2,1},{3,2},{4,7},{5,4},{6,5},{7,6},{8,11},{9,8},{10,9... | collective-permute-start | bytes 2457608 | tf_op jit(solution)/shard_map/ppermute | solution.py:233
  166.5 1.2 copy-start.3
  167.8 33.9 %collective-permute-start.7 = (f32[1,50,32,128]{3,2,1,0:T(8,128)S(1)}, f32[1,50,32,128]{3,2,1,0:T(8,128)}, u32[]{:S(2)}, u32[]{:S(2)}) collective-permute-start(f32[1,50,32,128]{3,2,1,0:T(8,128)S(1)} %slice.22), channel_id=1, source_target_pairs={{0,1},{1,2},{2,3},{3,0},{4,5},{5,6},{6,7},{7,4},{8,9},{9,10},{10,1... | collective-permute-start | bytes 2457608 | tf_op jit(solution)/shard_map/ppermute | solution.py:232
  167.8 1.2 copy-start.5
  170.0 31.6 %collective-permute-start.9 = (f32[1,50,32,128]{3,2,1,0:T(8,128)}, f32[1,50,32,128]{3,2,1,0:T(8,128)}, u32[]{:S(2)}, u32[]{:S(2)}) collective-permute-start(f32[1,50,32,128]{3,2,1,0:T(8,128)} %slice.23), channel_id=1, source_target_pairs={{0,3},{1,0},{2,1},{3,2},{4,7},{5,4},{6,5},{7,6},{8,11},{9,8},{10,9... | collective-permute-start | bytes 2457608 | tf_op jit(solution)/shard_map/ppermute | solution.py:233
  221.7 26.2 %all-to-all-start.3 = ((f32[16,32,256]{2,1,0:T(8,128)}), f32[16,32,256]{2,1,0:T(8,128)S(1)}, u32[]{:S(2)}, u32[]{:S(2)}) async-start(f32[16,32,256]{2,1,0:T(8,128)} %bitcast.56), calls=%async_computation.3 | async-start | bytes 1048576 | tf_op jit(solution)/shard_map/all_to_all | solution.py:252
  248.8 16.6 %all-to-all-start.4 = ((f32[16,32,256]{2,1,0:T(8,128)}), f32[16,32,256]{2,1,0:T(8,128)}, u32[]{:S(2)}, u32[]{:S(2)}) async-start(f32[16,32,256]{2,1,0:T(8,128)} %broadcast_in_dim.5), calls=%async_computation.4 | async-start | bytes 1048576 | tf_op jit(solution)/shard_map/all_to_all | solution.py:255
where the time goes:
time: 283 us; the launch traced here: 282 us
  waiting for transfers between devices  122 us (43%)
  Pallas kernels  63.2 us (22%)
  starting transfers between devices  44.6 us (16%)
  blocking collectives  25.4 us (9%)
  local copies, waits for them, and re-layouts  22.1 us (8%)
    ppermute x2, waiting for transfers between devices, per_device(): up = lax.ppermute(pair, 'col', col_perm(0, 1))  65.5 us
    pallas_call x4, Pallas kernels, prepare(): pl.pallas_call(prepare_kernel, grid_spec=pltpu.PrefetchScalarGridSpec(num...  31.8 us
    all_to_all x1, blocking collectives, per_device(): lax.all_to_all(piece, 'row', split_axis=0, concat_axis=0, tiled=True)  25.4 us
    ppermute x2, waiting for transfers between devices, per_device(): across = lax.ppermute(mine, 'col', col_perm(1, 0))  20.7 us
    pallas_call x1, Pallas kernels, apply(): pl.pallas_call(apply_kernel, grid_spec=pltpu.PrefetchScalarGridSpec(num_s...  16.4 us
    all_to_all x1, waiting for transfers between devices, per_device(): lax.all_to_all(piece, 'row', split_axis=0, concat_axis=0, tiled=True)  15.3 us
    all_to_all x1, starting transfers between devices, per_device(): lax.all_to_all(partial_value.reshape(ROWS, nb // ROWS, width), 'row', spl...  14.9 us
    all_to_all x1, waiting for transfers between devices, per_device(): lax.all_to_all(partial_value.reshape(ROWS, nb // ROWS, width), 'row', spl...  11.3 us
  transfers between devices with their start and end apart: 14, of which 9 were waited for; matrix products, arithmetic and copies ran while one was open for 7% of the time, Pallas kernels for 11%

commit v1 on v0

v1 whole, which is shorter than its diff:
```python
import functools

import jax
import jax.numpy as jnp
from jax import lax
from jax.experimental import pallas as pl
from jax.experimental.pallas import tpu as pltpu
from jax.sharding import PartitionSpec as P

TILE = 64
BLOCK = 2 * TILE
WINDOW = 50
SPAN = WINDOW * BLOCK
STEP = 5
PARTS = (25, 25)
ORDER = (0, 1, 3, 2)
ROWS = 16
F32, BF16 = jnp.float32, jnp.bfloat16
PARAMS = pltpu.CompilerParams(vmem_limit_bytes=60 * 2**20)


def col_perm(dl, dz):
    return [
        (low * 4 + z, (low ^ dl) * 4 + (z + dz) % 4) for low in range(2) for z in range(4)
    ]


def tile_kernel(y_ref, out_ref):
    lanes = lax.broadcasted_iota(jnp.int32, (y_ref.shape[0], BLOCK), 1)
    low = lanes < TILE
    for q in range(8):
        first = y_ref[:, q * BLOCK : (q + 1) * BLOCK]
        second = y_ref[:, 1024 + q * BLOCK : 1024 + (q + 1) * BLOCK]
        out_ref[2 * q, 0] = jnp.where(low, first, pltpu.roll(second, TILE, 1))
        out_ref[2 * q + 1, 0] = jnp.where(low, pltpu.roll(first, TILE, 1), second)


def cut_tiles(y_t):
    refl, height = y_t.shape
    steps = height // 2048
    return pl.pallas_call(
        tile_kernel,
        grid=(steps,),
        in_specs=[pl.BlockSpec((refl, 2048), lambda i: (0, i))],
        out_specs=pl.BlockSpec((ROWS, 1, refl, BLOCK), lambda i: (0, i, 0, 0)),
        out_shape=jax.ShapeDtypeStruct((ROWS, steps, refl, BLOCK), F32),
        name="cut_tiles",
        compiler_params=PARAMS,
    )(y_t)


def split(value):
    high = value.astype(BF16)
    return high, (value - high.astype(F32)).astype(BF16)


def prepare_kernel(skip, info, *refs):
    halves, (high, low, high_t, low_t, done) = refs[:2], refs[-5:]
    done[...] = jnp.zeros_like(done)
    rows = halves[0].shape[2]
    step = pl.program_id(0)
    lane = lax.broadcasted_iota(jnp.int32, (rows, BLOCK), 1)
    spread = (lane // TILE) * (ROWS * TILE) + lane % TILE
    spread = spread - lax.broadcasted_iota(jnp.int32, (rows, BLOCK), 0)
    band = info[3]
    for w in range(STEP):
        start = (info[0] + skip + step * STEP + w) * (BLOCK * ROWS) + info[1] * TILE - info[2]
        parts = []
        for half in range(2):
            away = spread + (start - info[4 + half])
            kept = jnp.where((away > 0) & (away < band), halves[half][0, w], 0.0)
            parts.append(jnp.where(away == 0, 1.0, kept))
        value = jnp.concatenate(parts, axis=0)
        at = slice(w * BLOCK, (w + 1) * BLOCK)
        high[:, at], low[:, at] = split(value)
        high_t[0, at, :], low_t[0, at, :] = split(value.T)


def prepare(info, halves, place, skip, height, count, before):
    arrays = [array for array, _ in halves]
    blocks, rows = arrays[0].shape[1:3]
    specs = [
        pl.BlockSpec((1, STEP, rows, BLOCK), functools.partial(lambda lead, i, s: (lead, i, 0, 0), lead))
        for _, lead in halves
    ]
    aliases = {3 + k: k for k in range(len(before))}
    specs += [pl.BlockSpec(memory_space=pl.ANY)] * len(before)
    wide = jax.ShapeDtypeStruct((count, SPAN), BF16)
    tall = jax.ShapeDtypeStruct((count // BLOCK, height, BLOCK), BF16)
    wide_spec = pl.BlockSpec((BLOCK, STEP * BLOCK), lambda i, s: (place, i + skip // STEP))
    tall_spec = pl.BlockSpec(
        (pl.Element(1), pl.Element(STEP * BLOCK), pl.Element(BLOCK)),
        lambda i, s: (place, pl.multiple_of((s[0] + skip + i * STEP) * BLOCK, BLOCK), 0),
    )
    done = jax.ShapeDtypeStruct((8, BLOCK), F32)
    done_spec = pl.BlockSpec((8, BLOCK), lambda i, s: (0, 0))
    return pl.pallas_call(
        functools.partial(prepare_kernel, skip),
        grid_spec=pltpu.PrefetchScalarGridSpec(
            num_scalar_prefetch=1,
            grid=(blocks // STEP,),
            in_specs=specs,
            out_specs=[wide_spec, wide_spec, tall_spec, tall_spec, done_spec],
        ),
        out_shape=[wide, wide, tall, tall, done],
        input_output_aliases=aliases,
        name="prepare",
        compiler_params=PARAMS,
        cost_estimate=pl.CostEstimate(flops=10**9, bytes_accessed=10**7, transcendentals=0),
    )(info, *arrays, *before)


def dot(a, b):
    return jnp.dot(a, b, preferred_element_type=F32)


def project_kernel(info, v_ref, high_ref, low_ref, out):
    @pl.when(pl.program_id(0) == 0)
    def _():
        out[...] = jnp.zeros_like(out)

    v_high, v_low = split(v_ref[...])
    high = high_ref[...]
    out[...] += dot(high, v_high) + dot(low_ref[...], v_high) + dot(high, v_low)


def project(info, cyc_v, high, low):
    width, count = cyc_v.shape[1], high.shape[0]
    rows = 2 * STEP * BLOCK
    wide = pl.BlockSpec((count, rows), lambda i, s: (0, i))
    window = pl.BlockSpec(
        (pl.Element(rows), pl.Element(width)),
        lambda i, s: (pl.multiple_of(s[0] * BLOCK + i * rows, BLOCK), 0),
    )
    return pl.pallas_call(
        project_kernel,
        grid_spec=pltpu.PrefetchScalarGridSpec(
            num_scalar_prefetch=1,
            grid=(SPAN // rows,),
            in_specs=[window, wide, wide],
            out_specs=pl.BlockSpec((count, width), lambda i, s: (0, 0)),
        ),
        out_shape=jax.ShapeDtypeStruct((count, width), F32),
        name="project",
        compiler_params=PARAMS,
        cost_estimate=pl.CostEstimate(flops=6 * count * SPAN * width, bytes_accessed=2 * 10**7, transcendentals=0),
    )(info, cyc_v, high, low)


def apply_kernel(info, v_ref, t_ref, p_ref, high_ref, low_ref, out, w_high, w_low):
    step = pl.program_id(0)
    rows = v_ref.shape[0]

    @pl.when(step == 0)
    def _():
        t_high, t_low = split(t_ref[...])
        p_high, p_low = split(p_ref[...])
        weights = dot(t_high, p_high) + dot(t_low, p_high) + dot(t_high, p_low)
        w_high[...], w_low[...] = split(weights)

    start = info[0] * BLOCK - step * rows
    touched = (start < rows) & (start + SPAN > 0)

    @pl.when(touched)
    def _():
        high = jnp.concatenate([high_ref[g] for g in range(4)], axis=1)
        low = jnp.concatenate([low_ref[g] for g in range(4)], axis=1)
        change = dot(high, w_high[...]) + dot(low, w_high[...]) + dot(high, w_low[...])
        at = lax.broadcasted_iota(jnp.int32, change.shape, 0) - start
        value = v_ref[...]
        out[...] = jnp.where((at >= 0) & (at < SPAN), value - change, value)

    @pl.when(jnp.logical_not(touched))
    def _():
        out[...] = v_ref[...]


def apply(info, cyc_v, t_rel, products, high, low):
    nb, (height, width) = high.shape[0] * BLOCK, cyc_v.shape
    rows = 8 * BLOCK
    tall = pl.BlockSpec((nb // BLOCK, rows, BLOCK), lambda i, s: (0, i, 0))
    plain = pl.BlockSpec((rows, width), lambda i, s: (i, 0))
    return pl.pallas_call(
        apply_kernel,
        grid_spec=pltpu.PrefetchScalarGridSpec(
            num_scalar_prefetch=1,
            grid=(height // rows,),
            in_specs=[
                plain,
                pl.BlockSpec((nb, nb), lambda i, s: (0, 0)),
                pl.BlockSpec((nb, width), lambda i, s: (0, 0)),
            ]
            + [tall] * 2,
            out_specs=plain,
            scratch_shapes=[pltpu.VMEM((nb, width), BF16)] * 2,
        ),
        out_shape=jax.ShapeDtypeStruct(cyc_v.shape, F32),
        name="apply",
        compiler_params=PARAMS,
        cost_estimate=pl.CostEstimate(flops=6 * 512 * SPAN * 256, bytes_accessed=3 * 10**7, transcendentals=0),
    )(info, cyc_v, t_rel, products, high, low)


def row_perm(dx, dy, dc):
    return [
        (x * 8 + y * 2 + c, (x ^ dx) * 8 + ((y + dy) % 4) * 2 + (c ^ dc))
        for x in range(2)
        for y in range(4)
        for c in range(2)
    ]


def sum_over_rows(value, position):
    core_perm, x_perm = row_perm(0, 0, 1), row_perm(1, 0, 0)
    cc, xh = position % 2, position // 8

    def halve(value, bit, perm):
        n = value.shape[0] // 2
        keep = lax.dynamic_slice_in_dim(value, bit * n, n, 0)
        give = lax.dynamic_slice_in_dim(value, (1 - bit) * n, n, 0)
        return keep + lax.ppermute(give, "row", perm)

    def join(value, bit, perm):
        other = lax.ppermute(value, "row", perm)
        first, second = jnp.where(bit == 0, value, other), jnp.where(bit == 0, other, value)
        return jnp.concatenate([first, second])

    value = halve(halve(value, cc, core_perm), xh, x_perm)
    value = value + sum(lax.ppermute(value, "row", row_perm(0, dy, 0)) for dy in (1, 2, 3))
    return join(join(value, xh, x_perm), cc, core_perm)


def per_device(vectors, reflectors, tmat, offset, band):
    height, width = vectors.shape
    refl = reflectors.shape[1]
    nb = 8 * refl
    position = lax.axis_index("row")
    place = lax.axis_index("col")
    xl, zz = place // 4, place % 4
    w0 = jnp.clip(offset[0] // (BLOCK * ROWS), 0, height // BLOCK - WINDOW)

    cut = lax.all_to_all(cut_tiles(reflectors.T), "row", split_axis=0, concat_axis=0, tiled=True)
    cut = cut.reshape(height // BLOCK, refl, BLOCK)
    skips = [sum(PARTS[:k]) for k in range(len(PARTS))]
    mine = lax.dynamic_slice_in_dim(cut, w0, WINDOW, 0)
    across = lax.ppermute(mine, "col", col_perm(1, 0))
    pairs = [jnp.stack([mine[k : k + n], across[k : k + n]]) for k, n in zip(skips, PARTS)]

    source = vectors.reshape(height // (ROWS * TILE), ROWS, TILE, width).transpose(1, 0, 2, 3)
    source, _ = lax.optimization_barrier((source, across))
    cyc_v = lax.all_to_all(source, "row", split_axis=0, concat_axis=0, tiled=True).reshape(height, width)

    infos, ids = {}, []
    for g in ORDER:
        base = ((zz + g) % 4) * refl
        starts = [(xl ^ half) * 4 * refl + base for half in range(2)]
        infos[g] = jnp.stack([w0, position, offset[0], band[0], *starts]).astype(jnp.int32)
        ids += [start + jnp.arange(refl) for start in starts]
    ids = jnp.concatenate(ids)
    t_rel = tmat[ids][:, ids]
    infos[0] = infos[0] + (t_rel[0, 0] * 0.0).astype(jnp.int32)

    ready = ()

    def arrive(k, g, halves):
        nonlocal ready
        *ready, done = prepare(infos[g], halves, ORDER.index(g), skips[k], height, nb, ready)
        return done

    def forward(up, down, done):
        zero = sum(token[0, 0] for token in done)
        far0 = lax.ppermute(up[:1] + zero, "col", col_perm(0, 1))
        far1 = lax.ppermute(down[1:] + zero, "col", col_perm(0, 3))
        return (far0, 0), (far1, 0)

    both = [
        (lax.ppermute(pair, "col", col_perm(0, 1)), lax.ppermute(pair, "col", col_perm(0, 3)))
        for pair in pairs
    ]
    done = [arrive(k, 0, ((pair, 0), (pair, 1))) for k, pair in enumerate(pairs)]
    fars = []
    for k, (up, down) in enumerate(both):
        fars.append(forward(up, down, done))
        done = [arrive(k, 1, ((down, 0), (down, 1))), arrive(k, 3, ((up, 0), (up, 1)))]
    info = w0[None].astype(jnp.int32)
    for k in range(len(PARTS)):
        arrive(k, 2, fars[k])
    high, low, high_t, low_t = ready
    partial_value = project(info, cyc_v, high, low)
    products = sum_over_rows(partial_value, position)
    return apply(info, cyc_v, t_rel, products, high_t, low_t)


def solution(mesh):
    placed = (P("row", "col"), P("row", "col"), P(), P(), P())
    return jax.shard_map(
        per_device, mesh=mesh, in_specs=placed, out_specs=P("row", "col"), check_vma=False
    )
```

time: 283 us -> 273 us (0.965)
  blocking collectives: 25.4 us -> 0 us
  waiting for transfers between devices: 122 us -> 101 us
  Pallas kernels: 63.2 us -> 77.1 us
  other arithmetic: 2.64 us -> 11 us
  local copies, waits for them, and re-layouts: 22.1 us -> 28.9 us
  starting transfers between devices: 44.6 us -> 48.4 us
  between operations: 1.5 us -> 4.71 us
    all_to_all x1 -> x0, blocking collectives: 25.4 us -> none  [per_device(): lax.all_to_all(piece, 'row', split_axis=0, concat_axis=0, tiled=True)]
    ppermute x8 -> x15, waiting for transfers between devices: 67.4 us -> 45.7 us  [the longest x2 18.2 us: per_device(): lax.ppermute(pair, 'col', col_perm(0, 3))]
    ppermute x8 -> x15, starting transfers between devices: 11 us -> 30.1 us  [the longest x2 7 us: forward(): far1 = lax.ppermute(down[1:] + zero, 'col', col_perm(0, 3))]
    all_to_all x3 -> x1, starting transfers between devices: 24.6 us -> 8.45 us  [per_device(): lax.all_to_all(cut_tiles(reflectors.T), 'row', split_axis=0, concat_axis=...]
    pallas_call x4 -> x8, Pallas kernels: 31.8 us -> 45.9 us  [prepare(): pl.pallas_call(functools.partial(prepare_kernel, skip), grid_spec=pltpu.P...]
    add x0 -> x8, other arithmetic: none -> 7.33 us  [the longest x2 3.36 us: forward(): far1 = lax.ppermute(down[1:] + zero, 'col', col_perm(0, 3))]
    ppermute x2 -> x1, waiting for transfers between devices: 20.7 us -> 27.6 us  [per_device(): across = lax.ppermute(mine, 'col', col_perm(1, 0))]
    all_to_all x3 -> x1, waiting for transfers between devices: 33 us -> 27.8 us  [per_device(): lax.all_to_all(cut_tiles(reflectors.T), 'row', split_axis=0, concat_axis=...]
  transfers between devices with their start and end apart: 14 -> 18, of which waited for: 9 -> 13; matrix products, arithmetic and copies ran while one was open for 7% -> 13% of each run, Pallas kernels for 11% -> 17%
where the time goes in v1:
time: 273 us; the launch traced here: 271 us
  waiting for transfers between devices  101 us (37%)
  Pallas kernels  77.1 us (28%)
  starting transfers between devices  48.4 us (18%)
  local copies, waits for them, and re-layouts  28.9 us (11%)
  other arithmetic  11 us (4%)
  between operations  4.71 us (2%)
    pallas_call x8, Pallas kernels, prepare(): pl.pallas_call(functools.partial(prepare_kernel, skip), grid_spec=pltpu.P...  45.9 us
    all_to_all x1, waiting for transfers between devices, per_device(): lax.all_to_all(cut_tiles(reflectors.T), 'row', split_axis=0, concat_axis=...  27.8 us
    ppermute x1, waiting for transfers between devices, per_device(): across = lax.ppermute(mine, 'col', col_perm(1, 0))  27.6 us
    ppermute x2, waiting for transfers between devices, per_device(): lax.ppermute(pair, 'col', col_perm(0, 3))  18.2 us
    pallas_call x1, Pallas kernels, apply(): pl.pallas_call(apply_kernel, grid_spec=pltpu.PrefetchScalarGridSpec(num_s...  16.2 us
    pallas_call x1, Pallas kernels, project(): pl.pallas_call(project_kernel, grid_spec=pltpu.PrefetchScalarGridSpec(num...  10.8 us
    all_to_all x1, starting transfers between devices, per_device(): lax.all_to_all(source, 'row', split_axis=0, concat_axis=0, tiled=True)  8.76 us
    ppermute x2, waiting for transfers between devices, forward(): far1 = lax.ppermute(down[1:] + zero, 'col', col_perm(0, 3))  8.73 us
  transfers between devices with their start and end apart: 18, of which 13 were waited for; matrix products, arithmetic and copies ran while one was open for 13% of the time, Pallas kernels for 17%

profile of v1, /device:TPU:1, one launch (start us, length us, event | category | flops | bytes accessed | tf_op | source)
XLA Modules:
  0.0 271.2 jit_solution(4900863735701018498)
XLA Ops:
  0.0 4.2 %cut_tiles.1 = f32[16,4,64,128]{3,2,1,0:T(8,128)} custom-call(f32[64,8192]{1,0:T(8,128)} %bitcast.57), custom_call_target="tpu_custom_call" | custom-call | tf_op jit(solution)/shard_map/cut_tiles/pallas_call | solution.py:41
  4.2 8.4 %all-to-all-start = ((f32[16,4,64,128]{3,2,1,0:T(8,128)}), f32[16,4,64,128]{3,2,1,0:T(8,128)S(1)}, u32[]{:S(2)}, u32[]{:S(2)}) async-start(f32[16,4,64,128]{3,2,1,0:T(8,128)} %cut_tiles.1), calls=%async_computation | async-start | bytes 4194304 | tf_op jit(solution)/shard_map/all_to_all | solution.py:242
  13.3 27.8 %all-to-all-done = f32[16,4,64,128]{3,2,1,0:T(8,128)S(1)} async-done(((f32[16,4,64,128]{3,2,1,0:T(8,128)}), f32[16,4,64,128]{3,2,1,0:T(8,128)S(1)}, u32[]{:S(2)}, u32[]{:S(2)}) %all-to-all-start) | async-done | bytes 2097184 | tf_op jit(solution)/shard_map/all_to_all | solution.py:242
  42.4 7.9 %copy.38 = f32[8,16,64,256]{3,2,0,1:T(8,128)} copy(f32[8,16,64,256]{3,2,1,0:T(8,128)} %bitcast.54) | data formatting | bytes 16777216 | tf_op jit(solution)/shard_map/reshape | solution.py:249
  50.2 27.6 %collective-permute-done = f32[50,64,128]{2,1,0:T(8,128)} collective-permute-done((f32[50,64,128]{2,1,0:T(8,128)S(1)}, f32[50,64,128]{2,1,0:T(8,128)}, u32[]{:S(2)}, u32[]{:S(2)}) %collective-permute-start) | collective-permute-done | bytes 1638432 | tf_op jit(solution)/shard_map/ppermute | solution.py:246
  77.9 8.8 %all-to-all-start.1 = ((f32[16,8,64,256]{3,2,1,0:T(8,128)}), f32[16,8,64,256]{3,2,1,0:T(8,128)}, u32[]{:S(2)}, u32[]{:S(2)}) async-start(f32[16,8,64,256]{3,2,1,0:T(8,128)} %bitcast.51), calls=%async_computation.1 | async-start | bytes 16777216 | tf_op jit(solution)/shard_map/all_to_all | solution.py:251
  91.6 3.8 %collective-permute-start.2 = (f32[2,25,64,128]{3,2,1,0:T(8,128)}, f32[2,25,64,128]{3,2,1,0:T(8,128)}, u32[]{:S(2)}, u32[]{:S(2)}) collective-permute-start(f32[2,25,64,128]{3,2,1,0:T(8,128)} %pad_maximum_fusion.1.refs_0_.refs_1_), channel_id=1, source_target_pairs={{0,3},{1,0},{2,1},{3,2},{4,7},{5,4},{6,5},{7,6},{8,11},{9,8},{10,9... | collective-permute-start | bytes 4915208 | tf_op jit(solution)/shard_map/ppermute | solution.py:277
  111.2 5.8 %prepare.8 = (bf16[512,6400]{1,0:T(8,128)(2,1)}, bf16[512,6400]{1,0:T(8,128)(2,1)}, bf16[4,8192,128]{2,1,0:T(8,128)(2,1)}, bf16[4,8192,128]{2,1,0:T(8,128)(2,1)}, f32[8,128]{1,0:T(8,128)}) custom-call(s32[6]{0:T(128)} %broadcast_add_fusion.info, f32[2,25,64,128]{3,2,1,0:T(8,128)} %pad_maximum_fusion.1.refs_0_.refs_1_, ...), custom_call_target="tpu_custom_call" | custom-call | flops 1000000000 | bytes 10000000 | tf_op jit(solution)/shard_map/prepare/pallas_call | solution.py:97
  117.0 5.7 %prepare.9 = (bf16[512,6400]{1,0:T(8,128)(2,1)}, bf16[512,6400]{1,0:T(8,128)(2,1)}, bf16[4,8192,128]{2,1,0:T(8,128)(2,1)}, bf16[4,8192,128]{2,1,0:T(8,128)(2,1)}, f32[8,128]{1,0:T(8,128)}) custom-call(s32[6]{0:T(128)} %broadcast_add_fusion.info, ...), custom_call_target="tpu_custom_call", output_to_operand_aliasing={{0}: (3, {}), {1}: (4, {}), {2}: (5, {}), {3}: (6, {})} | custom-call | flops 1000000000 | bytes 10000000 | tf_op jit(solution)/shard_map/prepare/pallas_call | solution.py:97
  126.4 4.3 %collective-permute-done.2.refs_0_.refs_1_ = f32[2,25,64,128]{3,2,1,0:T(8,128)} collective-permute-done((f32[2,25,64,128]{3,2,1,0:T(8,128)}, f32[2,25,64,128]{3,2,1,0:T(8,128)}, u32[]{:S(2)}, u32[]{:S(2)}) %collective-permute-start.2) | collective-permute-done | bytes 1638432 | tf_op jit(solution)/shard_map/ppermute | solution.py:277
  131.9 3.5 %collective-permute-start.8 = (f32[1,25,64,128]{3,2,1,0:T(8,128)S(1)}, f32[1,25,64,128]{3,2,1,0:T(8,128)}, u32[]{:S(2)}, u32[]{:S(2)}) collective-permute-start(f32[1,25,64,128]{3,2,1,0:T(8,128)S(1)} %slice_add_fusion), channel_id=1, source_target_pairs={{0,3},{1,0},{2,1},{3,2},{4,7},{5,4},{6,5},{7,6},{8,11},{9,8},{10,9... | collective-permute-start | bytes 2457608 | tf_op jit(solution)/shard_map/ppermute | solution.py:273
  136.7 5.7 %prepare.10 = (bf16[512,6400]{1,0:T(8,128)(2,1)}, bf16[512,6400]{1,0:T(8,128)(2,1)}, bf16[4,8192,128]{2,1,0:T(8,128)(2,1)}, bf16[4,8192,128]{2,1,0:T(8,128)(2,1)}, f32[8,128]{1,0:T(8,128)}) custom-call(s32[6]{0:T(128)} %stack.73.info, ...), custom_call_target="tpu_custom_call", output_to_operand_aliasing={{0}: (3, {}), {1}: (4, {}), {2}: (5, {}), {3}: (6, {})} | custom-call | flops 1000000000 | bytes 10000000 | tf_op jit(solution)/shard_map/prepare/pallas_call | solution.py:97
  142.4 5.7 %prepare.11 = (bf16[512,6400]{1,0:T(8,128)(2,1)}, bf16[512,6400]{1,0:T(8,128)(2,1)}, bf16[4,8192,128]{2,1,0:T(8,128)(2,1)}, bf16[4,8192,128]{2,1,0:T(8,128)(2,1)}, f32[8,128]{1,0:T(8,128)}) custom-call(s32[6]{0:T(128)} %stack.82.info, ...), custom_call_target="tpu_custom_call", output_to_operand_aliasing={{0}: (3, {}), {1}: (4, {}), {2}: (5, {}), {3}: (6, {})} | custom-call | flops 1000000000 | bytes 10000000 | tf_op jit(solution)/shard_map/prepare/pallas_call | solution.py:97
  151.8 13.9 %collective-permute-done.5.refs_0_.refs_1_ = f32[2,25,64,128]{3,2,1,0:T(8,128)} collective-permute-done((f32[2,25,64,128]{3,2,1,0:T(8,128)S(1)}, f32[2,25,64,128]{3,2,1,0:T(8,128)}, u32[]{:S(2)}, u32[]{:S(2)}) %collective-permute-start.5) | collective-permute-done | bytes 1638432 | tf_op jit(solution)/shard_map/ppermute | solution.py:277
  167.9 3.5 %collective-permute-start.6 = (f32[1,25,64,128]{3,2,1,0:T(8,128)}, f32[1,25,64,128]{3,2,1,0:T(8,128)}, u32[]{:S(2)}, u32[]{:S(2)}) collective-permute-start(f32[1,25,64,128]{3,2,1,0:T(8,128)} %slice_add_fusion.2), channel_id=1, source_target_pairs={{0,3},{1,0},{2,1},{3,2},{4,7},{5,4},{6,5},{7,6},{8,11},{9,8},{10,9... | collective-permute-start | bytes 2457608 | tf_op jit(solution)/shard_map/ppermute | solution.py:273
  173.4 5.8 %prepare.12 = (bf16[512,6400]{1,0:T(8,128)(2,1)}, bf16[512,6400]{1,0:T(8,128)(2,1)}, bf16[4,8192,128]{2,1,0:T(8,128)(2,1)}, bf16[4,8192,128]{2,1,0:T(8,128)(2,1)}, f32[8,128]{1,0:T(8,128)}) custom-call(s32[6]{0:T(128)} %stack.73.info, ...), custom_call_target="tpu_custom_call", output_to_operand_aliasing={{0}: (3, {}), {1}: (4, {}), {2}: (5, {}), {3}: (6, {})} | custom-call | flops 1000000000 | bytes 10000000 | tf_op jit(solution)/shard_map/prepare/pallas_call | solution.py:97
  179.1 5.7 %prepare.13 = (bf16[512,6400]{1,0:T(8,128)(2,1)}, bf16[512,6400]{1,0:T(8,128)(2,1)}, bf16[4,8192,128]{2,1,0:T(8,128)(2,1)}, bf16[4,8192,128]{2,1,0:T(8,128)(2,1)}, f32[8,128]{1,0:T(8,128)}) custom-call(s32[6]{0:T(128)} %stack.82.info, ...), custom_call_target="tpu_custom_call", output_to_operand_aliasing={{0}: (3, {}), {1}: (4, {}), {2}: (5, {}), {3}: (6, {})} | custom-call | flops 1000000000 | bytes 10000000 | tf_op jit(solution)/shard_map/prepare/pallas_call | solution.py:97
  186.5 5.7 %prepare.14 = (bf16[512,6400]{1,0:T(8,128)(2,1)}, bf16[512,6400]{1,0:T(8,128)(2,1)}, bf16[4,8192,128]{2,1,0:T(8,128)(2,1)}, bf16[4,8192,128]{2,1,0:T(8,128)(2,1)}, f32[8,128]{1,0:T(8,128)}) custom-call(s32[6]{0:T(128)} %stack.67.info, ...), custom_call_target="tpu_custom_call", output_to_operand_aliasing={{0}: (3, {}), {1}: (4, {}), {2}: (5, {}), {3}: (6, {})} | custom-call | flops 1000000000 | bytes 10000000 | tf_op jit(solution)/shard_map/prepare/pallas_call | solution.py:97
  192.2 8.7 %collective-permute-done.6.refs_1_ = f32[1,25,64,128]{3,2,1,0:T(8,128)} collective-permute-done((f32[1,25,64,128]{3,2,1,0:T(8,128)}, f32[1,25,64,128]{3,2,1,0:T(8,128)}, u32[]{:S(2)}, u32[]{:S(2)}) %collective-permute-start.6) | collective-permute-done | bytes 819232 | tf_op jit(solution)/shard_map/ppermute | solution.py:273
  204.8 5.7 %prepare.15 = (bf16[512,6400]{1,0:T(8,128)(2,1)}, bf16[512,6400]{1,0:T(8,128)(2,1)}, bf16[4,8192,128]{2,1,0:T(8,128)(2,1)}, bf16[4,8192,128]{2,1,0:T(8,128)(2,1)}, f32[8,128]{1,0:T(8,128)}) custom-call(s32[6]{0:T(128)} %stack.67.info, f32[1,25,64,128]{3,2,1,0:T(8,128)} %copy-done.5, ...), custom_call_target="tpu_custom_call", output_to_operand_aliasing={{0}: (3, {}), {1}: (4, {}), {2}: (5, {}), {3}: (6, {})} | custom-call | flops 1000000000 | bytes 10000000 | tf_op jit(solution)/shard_map/prepare/pallas_call | solution.py:97
  210.6 10.8 %project.1 = f32[512,256]{1,0:T(8,128)} custom-call(s32[1]{0:T(128)} %bitcast.1.info, f32[8192,256]{1,0:T(8,128)} %bitcast.6.v_ref, bf16[512,6400]{1,0:T(8,128)(2,1)} %get-tuple-element.75.high_ref, bf16[512,6400]{1,0:T(8,128)(2,1)} %get-tuple-element.76.low_ref), custom_call_target="tpu_custom_call" | custom-call | flops 5033164800 | bytes 20000000 | tf_op jit(solution)/shard_map/project/pallas_call | solution.py:135
  234.6 4.4 %collective-permute-start.12 = (f32[128,256]{1,0:T(8,128)S(1)}, f32[128,256]{1,0:T(8,128)S(1)}, u32[]{:S(2)}, u32[]{:S(2)}) collective-permute-start(f32[128,256]{1,0:T(8,128)S(1)} %dynamic-slice_add_fusion.1), channel_id=1, source_target_pairs={{0,32},{8,40},{16,48},{24,56},{32,0},{40,8},{48,16},{56,24},{64,96... | collective-permute-start | bytes 393224 | tf_op jit(solution)/shard_map/ppermute | solution.py:229
  240.9 3.7 %collective-permute-done.12 = f32[128,256]{1,0:T(8,128)S(1)} collective-permute-done((f32[128,256]{1,0:T(8,128)S(1)}, f32[128,256]{1,0:T(8,128)S(1)}, u32[]{:S(2)}, u32[]{:S(2)}) %collective-permute-start.12) | collective-permute-done | bytes 131104 | tf_op jit(solution)/shard_map/ppermute | solution.py:229
  255.0 16.2 %apply.1 = f32[8192,256]{1,0:T(8,128)} custom-call(s32[1]{0:T(128)} %bitcast.1.info, f32[8192,256]{1,0:T(8,128)} %bitcast.6.v_ref, f32[512,512]{1,0:T(8,128)} %bitcast.56, f32[512,256]{1,0:T(8,128)} %pad_maximum_fusion.2.p_ref, bf16[4,8192,128]{2,1,0:T(8,128)(2,1)} %get-tuple-element.77.high_ref, bf16[4,8192,128]{2,1,0:T(8,128)(2,1)} %get-tuple-element.78.low_ref), custom_call_target="tpu_custom_call" | custom-call | flops 5033164800 | bytes 30000000 | tf_op jit(solution)/shard_map/apply/pallas_call | solution.py:183
  (75 shorter events, 63.1 us)
Async XLA Ops:
  0.0 99.6 %copy-start = (f32[512,512]{1,0:T(8,128)S(1)}, f32[512,512]{1,0:T(8,128)}, u32[]{:S(2)}) copy-start(f32[512,512]{1,0:T(8,128)} %param.7) | copy-start | bytes 3145732
  4.2 36.9 %all-to-all-start = ((f32[16,4,64,128]{3,2,1,0:T(8,128)}), f32[16,4,64,128]{3,2,1,0:T(8,128)S(1)}, u32[]{:S(2)}, u32[]{:S(2)}) async-start(f32[16,4,64,128]{3,2,1,0:T(8,128)} %cut_tiles.1), calls=%async_computation | async-start | bytes 4194304 | tf_op jit(solution)/shard_map/all_to_all | solution.py:242
  41.3 36.6 %collective-permute-start = (f32[50,64,128]{2,1,0:T(8,128)S(1)}, f32[50,64,128]{2,1,0:T(8,128)}, u32[]{:S(2)}, u32[]{:S(2)}) collective-permute-start(f32[50,64,128]{2,1,0:T(8,128)S(1)} %constant_dynamic-slice_fusion.2), channel_id=1, source_target_pairs={{0,4},{1,5},{2,6},{3,7},{4,0},{5,1},{6,2},{7,3},{8,12},{9,13},{10,... | collective-permute-start | bytes 4915208 | tf_op jit(solution)/shard_map/ppermute | solution.py:246
  77.9 132.7 %all-to-all-start.1 = ((f32[16,8,64,256]{3,2,1,0:T(8,128)}), f32[16,8,64,256]{3,2,1,0:T(8,128)}, u32[]{:S(2)}, u32[]{:S(2)}) async-start(f32[16,8,64,256]{3,2,1,0:T(8,128)} %bitcast.51), calls=%async_computation.1 | async-start | bytes 16777216 | tf_op jit(solution)/shard_map/all_to_all | solution.py:251
  87.6 7.7 %copy-start.4 = (f32[1,25,64,128]{3,2,1,0:T(8,128)S(1)}, f32[1,25,64,128]{3,2,1,0:T(8,128)}, u32[]{:S(2)}) copy-start(f32[1,25,64,128]{3,2,1,0:T(8,128)} %get-tuple-element.80) | copy-start | bytes 2457604
  91.6 39.1 %collective-permute-start.2 = (f32[2,25,64,128]{3,2,1,0:T(8,128)}, f32[2,25,64,128]{3,2,1,0:T(8,128)}, u32[]{:S(2)}, u32[]{:S(2)}) collective-permute-start(f32[2,25,64,128]{3,2,1,0:T(8,128)} %pad_maximum_fusion.1.refs_0_.refs_1_), channel_id=1, source_target_pairs={{0,3},{1,0},{2,1},{3,2},{4,7},{5,4},{6,5},{7,6},{8,11},{9,8},{10,9... | collective-permute-start | bytes 4915208 | tf_op jit(solution)/shard_map/ppermute | solution.py:277
  95.3 40.1 %collective-permute-start.3 = (f32[2,25,64,128]{3,2,1,0:T(8,128)}, f32[2,25,64,128]{3,2,1,0:T(8,128)}, u32[]{:S(2)}, u32[]{:S(2)}) collective-permute-start(f32[2,25,64,128]{3,2,1,0:T(8,128)} %pad_maximum_fusion.1.refs_0_.refs_1_), channel_id=1, source_target_pairs={{0,1},{1,2},{2,3},{3,0},{4,5},{5,6},{6,7},{7,4},{8,9},{9,10},{10,1... | collective-permute-start | bytes 4915208 | tf_op jit(solution)/shard_map/ppermute | solution.py:277
  96.7 9.1 %copy-start.2 = (f32[2,25,64,128]{3,2,1,0:T(8,128)}, f32[2,25,64,128]{3,2,1,0:T(8,128)S(1)}, u32[]{:S(2)}) copy-start(f32[2,25,64,128]{3,2,1,0:T(8,128)S(1)} %pad_maximum_fusion.refs_0_.refs_1_) | copy-start | bytes 4915204
  96.7 69.0 %collective-permute-start.5 = (f32[2,25,64,128]{3,2,1,0:T(8,128)S(1)}, f32[2,25,64,128]{3,2,1,0:T(8,128)}, u32[]{:S(2)}, u32[]{:S(2)}) collective-permute-start(f32[2,25,64,128]{3,2,1,0:T(8,128)S(1)} %pad_maximum_fusion.refs_0_.refs_1_), channel_id=1, source_target_pairs={{0,3},{1,0},{2,1},{3,2},{4,7},{5,4},{6,5},{7,6},{8,11},{9,8},{10,9... | collective-permute-start | bytes 4915208 | tf_op jit(solution)/shard_map/ppermute | solution.py:277
  99.5 71.9 %collective-permute-start.1 = (f32[2,25,64,128]{3,2,1,0:T(8,128)S(1)}, f32[2,25,64,128]{3,2,1,0:T(8,128)}, u32[]{:S(2)}, u32[]{:S(2)}) collective-permute-start(f32[2,25,64,128]{3,2,1,0:T(8,128)S(1)} %pad_maximum_fusion.refs_0_.refs_1_), channel_id=1, source_target_pairs={{0,1},{1,2},{2,3},{3,0},{4,5},{5,6},{6,7},{7,4},{8,9},{9,10},{10,1... | collective-permute-start | bytes 4915208 | tf_op jit(solution)/shard_map/ppermute | solution.py:277
  107.4 15.4 %copy-start.3 = (f32[512,512]{0,1:T(8,128)}, f32[512,512]{0,1:T(8,128)S(1)}, u32[]{:S(2)}) copy-start(f32[512,512]{0,1:T(8,128)S(1)} %copy.36) | copy-start | bytes 3145732
  131.9 52.9 %collective-permute-start.8 = (f32[1,25,64,128]{3,2,1,0:T(8,128)S(1)}, f32[1,25,64,128]{3,2,1,0:T(8,128)}, u32[]{:S(2)}, u32[]{:S(2)}) collective-permute-start(f32[1,25,64,128]{3,2,1,0:T(8,128)S(1)} %slice_add_fusion), channel_id=1, source_target_pairs={{0,3},{1,0},{2,1},{3,2},{4,7},{5,4},{6,5},{7,6},{8,11},{9,8},{10,9... | collective-permute-start | bytes 2457608 | tf_op jit(solution)/shard_map/ppermute | solution.py:273
  136.6 49.8 %collective-permute-start.7 = (f32[1,25,64,128]{3,2,1,0:T(8,128)S(1)}, f32[1,25,64,128]{3,2,1,0:T(8,128)}, u32[]{:S(2)}, u32[]{:S(2)}) collective-permute-start(f32[1,25,64,128]{3,2,1,0:T(8,128)S(1)} %slice_add_fusion.1), channel_id=1, source_target_pairs={{0,1},{1,2},{2,3},{3,0},{4,5},{5,6},{6,7},{7,4},{8,9},{9,10},{10,1... | collective-permute-start | bytes 2457608 | tf_op jit(solution)/shard_map/ppermute | solution.py:272
  167.9 33.1 %collective-permute-start.6 = (f32[1,25,64,128]{3,2,1,0:T(8,128)}, f32[1,25,64,128]{3,2,1,0:T(8,128)}, u32[]{:S(2)}, u32[]{:S(2)}) collective-permute-start(f32[1,25,64,128]{3,2,1,0:T(8,128)} %slice_add_fusion.2), channel_id=1, source_target_pairs={{0,3},{1,0},{2,1},{3,2},{4,7},{5,4},{6,5},{7,6},{8,11},{9,8},{10,9... | collective-permute-start | bytes 2457608 | tf_op jit(solution)/shard_map/ppermute | solution.py:273
  172.6 31.3 %collective-permute-start.4 = (f32[1,25,64,128]{3,2,1,0:T(8,128)S(1)}, f32[1,25,64,128]{3,2,1,0:T(8,128)S(1)}, u32[]{:S(2)}, u32[]{:S(2)}) collective-permute-start(f32[1,25,64,128]{3,2,1,0:T(8,128)S(1)} %slice_add_fusion.3), channel_id=1, source_target_pairs={{0,1},{1,2},{2,3},{3,0},{4,5},{5,6},{6,7},{7,4},{8,9},{9,10},{10,1... | collective-permute-start | bytes 2457608 | tf_op jit(solution)/shard_map/ppermute | solution.py:272
  203.9 0.9 copy-start.5
  222.3 2.5 collective-permute-start.9
  225.9 6.3 %collective-permute-start.10 = (f32[128,256]{1,0:T(8,128)S(1)}, f32[128,256]{1,0:T(8,128)S(1)}, u32[]{:S(2)}, u32[]{:S(2)}) collective-permute-start(f32[128,256]{1,0:T(8,128)S(1)} %constant_dynamic-slice_fusion), channel_id=1, source_target_pairs={{0,64},{8,72},{16,80},{24,88},{32,96},{40,104},{48,112},{56,120},{... | collective-permute-start | bytes 393224 | tf_op jit(solution)/shard_map/ppermute | solution.py:221
  232.2 8.8 %collective-permute-start.11 = (f32[128,256]{1,0:T(8,128)S(1)}, f32[128,256]{1,0:T(8,128)S(1)}, u32[]{:S(2)}, u32[]{:S(2)}) collective-permute-start(f32[128,256]{1,0:T(8,128)S(1)} %dynamic-slice_add_fusion.1), channel_id=1, source_target_pairs={{0,16},{8,24},{16,32},{24,40},{32,48},{40,56},{48,0},{56,8},{64,80... | collective-permute-start | bytes 393224 | tf_op jit(solution)/shard_map/ppermute | solution.py:229
  234.6 10.1 %collective-permute-start.12 = (f32[128,256]{1,0:T(8,128)S(1)}, f32[128,256]{1,0:T(8,128)S(1)}, u32[]{:S(2)}, u32[]{:S(2)}) collective-permute-start(f32[128,256]{1,0:T(8,128)S(1)} %dynamic-slice_add_fusion.1), channel_id=1, source_target_pairs={{0,32},{8,40},{16,48},{24,56},{32,0},{40,8},{48,16},{56,24},{64,96... | collective-permute-start | bytes 393224 | tf_op jit(solution)/shard_map/ppermute | solution.py:229
  238.9 5.7 %collective-permute-start.13 = (f32[128,256]{1,0:T(8,128)S(1)}, f32[128,256]{1,0:T(8,128)S(1)}, u32[]{:S(2)}, u32[]{:S(2)}) collective-permute-start(f32[128,256]{1,0:T(8,128)S(1)} %dynamic-slice_add_fusion.1), channel_id=1, source_target_pairs={{0,48},{8,56},{16,0},{24,8},{32,16},{40,24},{48,32},{56,40},{64,11... | collective-permute-start | bytes 393224 | tf_op jit(solution)/shard_map/ppermute | solution.py:229
  244.7 5.4 %collective-permute-start.14 = (f32[128,256]{1,0:T(8,128)S(1)}, f32[128,256]{1,0:T(8,128)S(1)}, u32[]{:S(2)}, u32[]{:S(2)}) collective-permute-start(f32[128,256]{1,0:T(8,128)S(1)} %add_add_fusion), channel_id=1, source_target_pairs={{0,64},{8,72},{16,80},{24,88},{32,96},{40,104},{48,112},{56,120},{... | collective-permute-start | bytes 393224 | tf_op jit(solution)/shard_map/ppermute | solution.py:224
  250.1 4.0 %collective-permute-start.15 = (f32[256,256]{1,0:T(8,128)S(1)}, f32[256,256]{1,0:T(8,128)S(1)}, u32[]{:S(2)}, u32[]{:S(2)}) collective-permute-start(f32[256,256]{1,0:T(8,128)S(1)} %pad_maximum_fusion.3), channel_id=1, source_target_pairs={{0,8},{8,0},{16,24},{24,16},{32,40},{40,32},{48,56},{56,48},{64,72... | collective-permute-start | bytes 786440 | tf_op jit(solution)/shard_map/ppermute | solution.py:224
  255.0 16.2 %copy-start.1 = (f32[512,512]{1,0:T(8,128)S(1)}, f32[512,512]{1,0:T(8,128)}, u32[]{:S(2)}) copy-start(f32[512,512]{1,0:T(8,128)} %param.7) | copy-start | bytes 3145732

commit v2 on v1

--- a/solution.py
+++ b/solution.py
@@ -12,7 +12,7 @@
 WINDOW = 50
 SPAN = WINDOW * BLOCK
 STEP = 5
-PARTS = (25, 25)
+PARTS = (30, 20)
 ORDER = (0, 1, 3, 2)
 ROWS = 16
 F32, BF16 = jnp.float32, jnp.bfloat16
@@ -121,7 +121,8 @@
 
     v_high, v_low = split(v_ref[...])
     high = high_ref[...]
-    out[...] += dot(high, v_high) + dot(low_ref[...], v_high) + dot(high, v_low)
+    left = jnp.concatenate([high, low_ref[...], high], axis=1)
+    out[...] += dot(left, jnp.concatenate([v_high, v_high, v_low], axis=0))
 
 
 def project(info, cyc_v, high, low):
@@ -147,7 +148,7 @@
     )(info, cyc_v, high, low)
 
 
-def apply_kernel(info, v_ref, t_ref, p_ref, high_ref, low_ref, out, w_high, w_low):
+def apply_kernel(info, v_ref, t_ref, p_ref, high_ref, low_ref, out, w_all):
     step = pl.program_id(0)
     rows = v_ref.shape[0]
 
@@ -156,16 +157,17 @@
         t_high, t_low = split(t_ref[...])
         p_high, p_low = split(p_ref[...])
         weights = dot(t_high, p_high) + dot(t_low, p_high) + dot(t_high, p_low)
-        w_high[...], w_low[...] = split(weights)
+        w_high, w_low = split(weights)
+        w_all[...] = jnp.concatenate([w_high, w_high, w_low], axis=0)
 
     start = info[0] * BLOCK - step * rows
     touched = (start < rows) & (start + SPAN > 0)
 
     @pl.when(touched)
     def _():
-        high = jnp.concatenate([high_ref[g] for g in range(4)], axis=1)
-        low = jnp.concatenate([low_ref[g] for g in range(4)], axis=1)
-        change = dot(high, w_high[...]) + dot(low, w_high[...]) + dot(high, w_low[...])
+        high = [high_ref[g] for g in range(4)]
+        low = [low_ref[g] for g in range(4)]
+        change = dot(jnp.concatenate(high + low + high, axis=1), w_all[...])
         at = lax.broadcasted_iota(jnp.int32, change.shape, 0) - start
         value = v_ref[...]
         out[...] = jnp.where((at >= 0) & (at < SPAN), value - change, value)
@@ -178,7 +180,8 @@
 def apply(info, cyc_v, t_rel, products, high, low):
     nb, (height, width) = high.shape[0] * BLOCK, cyc_v.shape
     rows = 8 * BLOCK
-    tall = pl.BlockSpec((nb // BLOCK, rows, BLOCK), lambda i, s: (0, i, 0))
+    held = lambda i, s: jnp.clip(i, s[0] * BLOCK // rows, (s[0] * BLOCK + SPAN - 1) // rows)
+    tall = pl.BlockSpec((nb // BLOCK, rows, BLOCK), lambda i, s: (0, held(i, s), 0))
     plain = pl.BlockSpec((rows, width), lambda i, s: (i, 0))
     return pl.pallas_call(
         apply_kernel,
@@ -192,7 +195,7 @@
             ]
             + [tall] * 2,
             out_specs=plain,
-            scratch_shapes=[pltpu.VMEM((nb, width), BF16)] * 2,
+            scratch_shapes=[pltpu.VMEM((3 * nb, width), BF16)],
         ),
         out_shape=jax.ShapeDtypeStruct(cyc_v.shape, F32),
         name="apply",

time: 273 us -> 273 us (level)
  starting transfers between devices: 48.4 us -> 52.4 us
  waiting for transfers between devices: 101 us -> 98.1 us
    ppermute x3, starting transfers between devices: 6.75 us -> 11.7 us  [sum_over_rows(): lax.ppermute(value, 'row', row_perm(0, dy, 0))]
    ppermute x2, waiting for transfers between devices: 18.2 us -> 14 us  [per_device(): lax.ppermute(pair, 'col', col_perm(0, 3))]
  transfers between devices with their start and end apart: 18 -> 18, of which waited for: 13 -> 15; matrix products, arithmetic and copies ran while one was open for 13% -> 13% of each run, Pallas kernels for 17% -> 16%
where the time goes in v2:
time: 273 us; the launch traced here: 271 us
  waiting for transfers between devices  98.1 us (36%)
  Pallas kernels  75.4 us (28%)
  starting transfers between devices  52.4 us (19%)
  local copies, waits for them, and re-layouts  29.1 us (11%)
  other arithmetic  11.4 us (4%)
  between operations  4.67 us (2%)
    pallas_call x8, Pallas kernels, prepare(): pl.pallas_call(functools.partial(prepare_kernel, skip), grid_spec=pltpu.P...  44.4 us
    all_to_all x1, waiting for transfers between devices, per_device(): lax.all_to_all(cut_tiles(reflectors.T), 'row', split_axis=0, concat_axis=...  27.8 us
    ppermute x1, waiting for transfers between devices, per_device(): across = lax.ppermute(mine, 'col', col_perm(1, 0))  27.6 us
    pallas_call x1, Pallas kernels, apply(): pl.pallas_call(apply_kernel, grid_spec=pltpu.PrefetchScalarGridSpec(num_s...  16 us
    ppermute x2, waiting for transfers between devices, per_device(): lax.ppermute(pair, 'col', col_perm(0, 3))  14 us
    ppermute x3, starting transfers between devices, sum_over_rows(): lax.ppermute(value, 'row', row_perm(0, dy, 0))  11.7 us
    pallas_call x1, Pallas kernels, project(): pl.pallas_call(project_kernel, grid_spec=pltpu.PrefetchScalarGridSpec(num...  10.8 us
    all_to_all x1, starting transfers between devices, per_device(): lax.all_to_all(source, 'row', split_axis=0, concat_axis=0, tiled=True)  8.76 us
  transfers between devices with their start and end apart: 18, of which 15 were waited for; matrix products, arithmetic and copies ran while one was open for 13% of the time, Pallas kernels for 16%

profile of v2, /device:TPU:1, one launch (start us, length us, event | category | flops | bytes accessed | tf_op | source)
XLA Modules:
  0.0 271.0 jit_solution(16678204913827626876)
XLA Ops:
  0.0 4.2 %cut_tiles.1 = f32[16,4,64,128]{3,2,1,0:T(8,128)} custom-call(f32[64,8192]{1,0:T(8,128)} %bitcast.58), custom_call_target="tpu_custom_call" | custom-call | tf_op jit(solution)/shard_map/cut_tiles/pallas_call | solution.py:41
  4.2 8.4 %all-to-all-start = ((f32[16,4,64,128]{3,2,1,0:T(8,128)}), f32[16,4,64,128]{3,2,1,0:T(8,128)S(1)}, u32[]{:S(2)}, u32[]{:S(2)}) async-start(f32[16,4,64,128]{3,2,1,0:T(8,128)} %cut_tiles.1), calls=%async_computation | async-start | bytes 4194304 | tf_op jit(solution)/shard_map/all_to_all | solution.py:245
  13.3 27.8 %all-to-all-done = f32[16,4,64,128]{3,2,1,0:T(8,128)S(1)} async-done(((f32[16,4,64,128]{3,2,1,0:T(8,128)}), f32[16,4,64,128]{3,2,1,0:T(8,128)S(1)}, u32[]{:S(2)}, u32[]{:S(2)}) %all-to-all-start) | async-done | bytes 2097184 | tf_op jit(solution)/shard_map/all_to_all | solution.py:245
  42.4 7.9 %copy.38 = f32[8,16,64,256]{3,2,0,1:T(8,128)} copy(f32[8,16,64,256]{3,2,1,0:T(8,128)} %bitcast.55) | data formatting | bytes 16777216 | tf_op jit(solution)/shard_map/reshape | solution.py:252
  50.2 27.6 %collective-permute-done = f32[50,64,128]{2,1,0:T(8,128)} collective-permute-done((f32[50,64,128]{2,1,0:T(8,128)S(1)}, f32[50,64,128]{2,1,0:T(8,128)}, u32[]{:S(2)}, u32[]{:S(2)}) %collective-permute-start) | collective-permute-done | bytes 1638432 | tf_op jit(solution)/shard_map/ppermute | solution.py:249
  77.9 8.8 %all-to-all-start.1 = ((f32[16,8,64,256]{3,2,1,0:T(8,128)}), f32[16,8,64,256]{3,2,1,0:T(8,128)}, u32[]{:S(2)}, u32[]{:S(2)}) async-start(f32[16,8,64,256]{3,2,1,0:T(8,128)} %bitcast.51), calls=%async_computation.1 | async-start | bytes 16777216 | tf_op jit(solution)/shard_map/all_to_all | solution.py:254
  88.2 3.8 %collective-permute-start.2 = (f32[2,30,64,128]{3,2,1,0:T(8,128)S(1)}, f32[2,30,64,128]{3,2,1,0:T(8,128)}, u32[]{:S(2)}, u32[]{:S(2)}) collective-permute-start(f32[2,30,64,128]{3,2,1,0:T(8,128)S(1)} %pad_maximum_fusion.refs_0_.refs_1_), channel_id=1, source_target_pairs={{0,3},{1,0},{2,1},{3,2},{4,7},{5,4},{6,5},{7,6},{8,11},{9,8},{10,9... | collective-permute-start | bytes 5898248 | tf_op jit(solution)/shard_map/ppermute | solution.py:280
  109.8 6.4 %prepare.8 = (bf16[512,6400]{1,0:T(8,128)(2,1)}, bf16[512,6400]{1,0:T(8,128)(2,1)}, bf16[4,8192,128]{2,1,0:T(8,128)(2,1)}, bf16[4,8192,128]{2,1,0:T(8,128)(2,1)}, f32[8,128]{1,0:T(8,128)}) custom-call(s32[6]{0:T(128)} %broadcast_add_fusion.info, f32[2,30,64,128]{3,2,1,0:T(8,128)} %copy-done.2, f32[2,30,64,128]{3,2,1,0:T(8,128)} %copy-done.2), custom_call_target="tpu_custom_call" | custom-call | flops 1000000000 | bytes 10000000 | tf_op jit(solution)/shard_map/prepare/pallas_call | solution.py:97
  116.1 4.7 %prepare.9 = (bf16[512,6400]{1,0:T(8,128)(2,1)}, bf16[512,6400]{1,0:T(8,128)(2,1)}, bf16[4,8192,128]{2,1,0:T(8,128)(2,1)}, bf16[4,8192,128]{2,1,0:T(8,128)(2,1)}, f32[8,128]{1,0:T(8,128)}) custom-call(s32[6]{0:T(128)} %broadcast_add_fusion.info, ...), custom_call_target="tpu_custom_call", output_to_operand_aliasing={{0}: (3, {}), {1}: (4, {}), {2}: (5, {}), {3}: (6, {})} | custom-call | flops 1000000000 | bytes 10000000 | tf_op jit(solution)/shard_map/prepare/pallas_call | solution.py:97
  124.7 9.4 %collective-permute-done.2.refs_0_.refs_1_ = f32[2,30,64,128]{3,2,1,0:T(8,128)} collective-permute-done((f32[2,30,64,128]{3,2,1,0:T(8,128)S(1)}, f32[2,30,64,128]{3,2,1,0:T(8,128)}, u32[]{:S(2)}, u32[]{:S(2)}) %collective-permute-start.2) | collective-permute-done | bytes 1966112 | tf_op jit(solution)/shard_map/ppermute | solution.py:280
  141.2 6.3 %prepare.10 = (bf16[512,6400]{1,0:T(8,128)(2,1)}, bf16[512,6400]{1,0:T(8,128)(2,1)}, bf16[4,8192,128]{2,1,0:T(8,128)(2,1)}, bf16[4,8192,128]{2,1,0:T(8,128)(2,1)}, f32[8,128]{1,0:T(8,128)}) custom-call(s32[6]{0:T(128)} %stack.73.info, ...), custom_call_target="tpu_custom_call", output_to_operand_aliasing={{0}: (3, {}), {1}: (4, {}), {2}: (5, {}), {3}: (6, {})} | custom-call | flops 1000000000 | bytes 10000000 | tf_op jit(solution)/shard_map/prepare/pallas_call | solution.py:97
  147.6 6.4 %prepare.11 = (bf16[512,6400]{1,0:T(8,128)(2,1)}, bf16[512,6400]{1,0:T(8,128)(2,1)}, bf16[4,8192,128]{2,1,0:T(8,128)(2,1)}, bf16[4,8192,128]{2,1,0:T(8,128)(2,1)}, f32[8,128]{1,0:T(8,128)}) custom-call(s32[6]{0:T(128)} %stack.82.info, ...), custom_call_target="tpu_custom_call", output_to_operand_aliasing={{0}: (3, {}), {1}: (4, {}), {2}: (5, {}), {3}: (6, {})} | custom-call | flops 1000000000 | bytes 10000000 | tf_op jit(solution)/shard_map/prepare/pallas_call | solution.py:97
  157.7 4.6 %collective-permute-done.5.refs_0_.refs_1_ = f32[2,20,64,128]{3,2,1,0:T(8,128)} collective-permute-done((f32[2,20,64,128]{3,2,1,0:T(8,128)}, f32[2,20,64,128]{3,2,1,0:T(8,128)}, u32[]{:S(2)}, u32[]{:S(2)}) %collective-permute-start.5) | collective-permute-done | bytes 1310752 | tf_op jit(solution)/shard_map/ppermute | solution.py:280
  170.3 4.8 %prepare.12 = (bf16[512,6400]{1,0:T(8,128)(2,1)}, bf16[512,6400]{1,0:T(8,128)(2,1)}, bf16[4,8192,128]{2,1,0:T(8,128)(2,1)}, bf16[4,8192,128]{2,1,0:T(8,128)(2,1)}, f32[8,128]{1,0:T(8,128)}) custom-call(s32[6]{0:T(128)} %stack.73.info, ...), custom_call_target="tpu_custom_call", output_to_operand_aliasing={{0}: (3, {}), {1}: (4, {}), {2}: (5, {}), {3}: (6, {})} | custom-call | flops 1000000000 | bytes 10000000 | tf_op jit(solution)/shard_map/prepare/pallas_call | solution.py:97
  175.1 4.7 %prepare.13 = (bf16[512,6400]{1,0:T(8,128)(2,1)}, bf16[512,6400]{1,0:T(8,128)(2,1)}, bf16[4,8192,128]{2,1,0:T(8,128)(2,1)}, bf16[4,8192,128]{2,1,0:T(8,128)(2,1)}, f32[8,128]{1,0:T(8,128)}) custom-call(s32[6]{0:T(128)} %stack.82.info, ...), custom_call_target="tpu_custom_call", output_to_operand_aliasing={{0}: (3, {}), {1}: (4, {}), {2}: (5, {}), {3}: (6, {})} | custom-call | flops 1000000000 | bytes 10000000 | tf_op jit(solution)/shard_map/prepare/pallas_call | solution.py:97
  187.2 6.4 %prepare.14 = (bf16[512,6400]{1,0:T(8,128)(2,1)}, bf16[512,6400]{1,0:T(8,128)(2,1)}, bf16[4,8192,128]{2,1,0:T(8,128)(2,1)}, bf16[4,8192,128]{2,1,0:T(8,128)(2,1)}, f32[8,128]{1,0:T(8,128)}) custom-call(s32[6]{0:T(128)} %stack.67.info, f32[1,30,64,128]{3,2,1,0:T(8,128)} %copy-done.6, ...), custom_call_target="tpu_custom_call", output_to_operand_aliasing={{0}: (3, {}), {1}: (4, {}), {2}: (5, {}), {3}: (6, {})} | custom-call | flops 1000000000 | bytes 10000000 | tf_op jit(solution)/shard_map/prepare/pallas_call | solution.py:97
  193.6 3.7 %collective-permute-done.6.refs_1_ = f32[1,20,64,128]{3,2,1,0:T(8,128)} collective-permute-done((f32[1,20,64,128]{3,2,1,0:T(8,128)}, f32[1,20,64,128]{3,2,1,0:T(8,128)}, u32[]{:S(2)}, u32[]{:S(2)}) %collective-permute-start.6) | collective-permute-done | bytes 655392 | tf_op jit(solution)/shard_map/ppermute | solution.py:276
  200.5 4.7 %prepare.15 = (bf16[512,6400]{1,0:T(8,128)(2,1)}, bf16[512,6400]{1,0:T(8,128)(2,1)}, bf16[4,8192,128]{2,1,0:T(8,128)(2,1)}, bf16[4,8192,128]{2,1,0:T(8,128)(2,1)}, f32[8,128]{1,0:T(8,128)}) custom-call(s32[6]{0:T(128)} %stack.67.info, ...), custom_call_target="tpu_custom_call", output_to_operand_aliasing={{0}: (3, {}), {1}: (4, {}), {2}: (5, {}), {3}: (6, {})} | custom-call | flops 1000000000 | bytes 10000000 | tf_op jit(solution)/shard_map/prepare/pallas_call | solution.py:97
  206.1 10.8 %project.1 = f32[512,256]{1,0:T(8,128)} custom-call(s32[1]{0:T(128)} %bitcast.1.info, f32[8192,256]{1,0:T(8,128)} %bitcast.6.v_ref, bf16[512,6400]{1,0:T(8,128)(2,1)} %get-tuple-element.75.high_ref, bf16[512,6400]{1,0:T(8,128)(2,1)} %get-tuple-element.76.low_ref), custom_call_target="tpu_custom_call" | custom-call | flops 5033164800 | bytes 20000000 | tf_op jit(solution)/shard_map/project/pallas_call | solution.py:136
  223.5 3.7 %collective-permute-done.10 = f32[128,256]{1,0:T(8,128)S(1)} collective-permute-done((f32[128,256]{1,0:T(8,128)S(1)}, f32[128,256]{1,0:T(8,128)S(1)}, u32[]{:S(2)}, u32[]{:S(2)}) %collective-permute-start.10) | collective-permute-done | bytes 131104 | tf_op jit(solution)/shard_map/ppermute | solution.py:224
  227.2 7.3 %collective-permute-start.11 = (f32[128,256]{1,0:T(8,128)S(1)}, f32[128,256]{1,0:T(8,128)S(1)}, u32[]{:S(2)}, u32[]{:S(2)}) collective-permute-start(f32[128,256]{1,0:T(8,128)S(1)} %dynamic-slice_add_fusion.1), channel_id=1, source_target_pairs={{0,16},{8,24},{16,32},{24,40},{32,48},{40,56},{48,0},{56,8},{64,80... | collective-permute-start | bytes 393224 | tf_op jit(solution)/shard_map/ppermute | solution.py:232
  234.6 4.4 %collective-permute-start.12 = (f32[128,256]{1,0:T(8,128)S(1)}, f32[128,256]{1,0:T(8,128)S(1)}, u32[]{:S(2)}, u32[]{:S(2)}) collective-permute-start(f32[128,256]{1,0:T(8,128)S(1)} %dynamic-slice_add_fusion.1), channel_id=1, source_target_pairs={{0,32},{8,40},{16,48},{24,56},{32,0},{40,8},{48,16},{56,24},{64,96... | collective-permute-start | bytes 393224 | tf_op jit(solution)/shard_map/ppermute | solution.py:232
  240.9 3.7 %collective-permute-done.12 = f32[128,256]{1,0:T(8,128)S(1)} collective-permute-done((f32[128,256]{1,0:T(8,128)S(1)}, f32[128,256]{1,0:T(8,128)S(1)}, u32[]{:S(2)}, u32[]{:S(2)}) %collective-permute-start.12) | collective-permute-done | bytes 131104 | tf_op jit(solution)/shard_map/ppermute | solution.py:232
  255.0 16.0 %apply.1 = f32[8192,256]{1,0:T(8,128)} custom-call(s32[1]{0:T(128)} %bitcast.1.info, f32[8192,256]{1,0:T(8,128)} %bitcast.6.v_ref, f32[512,512]{1,0:T(8,128)} %bitcast.57, f32[512,256]{1,0:T(8,128)} %pad_maximum_fusion.2.p_ref, bf16[4,8192,128]{2,1,0:T(8,128)(2,1)} %get-tuple-element.77.high_ref, bf16[4,8192,128]{2,1,0:T(8,128)(2,1)} %get-tuple-element.78.low_ref), custom_call_target="tpu_custom_call" | custom-call | flops 5033164800 | bytes 30000000 | tf_op jit(solution)/shard_map/apply/pallas_call | solution.py:186
  (79 shorter events, 69.8 us)
Async XLA Ops:
  0.0 98.2 %copy-start = (f32[512,512]{1,0:T(8,128)S(1)}, f32[512,512]{1,0:T(8,128)}, u32[]{:S(2)}) copy-start(f32[512,512]{1,0:T(8,128)} %param.7) | copy-start | bytes 3145732
  4.2 36.9 %all-to-all-start = ((f32[16,4,64,128]{3,2,1,0:T(8,128)}), f32[16,4,64,128]{3,2,1,0:T(8,128)S(1)}, u32[]{:S(2)}, u32[]{:S(2)}) async-start(f32[16,4,64,128]{3,2,1,0:T(8,128)} %cut_tiles.1), calls=%async_computation | async-start | bytes 4194304 | tf_op jit(solution)/shard_map/all_to_all | solution.py:245
  41.1 45.5 %copy-start.3 = (f32[16,4,64,128]{3,2,1,0:T(8,128)}, f32[16,4,64,128]{3,2,1,0:T(8,128)S(1)}, u32[]{:S(2)}) copy-start(f32[16,4,64,128]{3,2,1,0:T(8,128)S(1)} %all-to-all-done) | copy-start | bytes 6291460
  41.3 36.6 %collective-permute-start = (f32[50,64,128]{2,1,0:T(8,128)S(1)}, f32[50,64,128]{2,1,0:T(8,128)}, u32[]{:S(2)}, u32[]{:S(2)}) collective-permute-start(f32[50,64,128]{2,1,0:T(8,128)S(1)} %constant_dynamic-slice_fusion.2), channel_id=1, source_target_pairs={{0,4},{1,5},{2,6},{3,7},{4,0},{5,1},{6,2},{7,3},{8,12},{9,13},{10,... | collective-permute-start | bytes 4915208 | tf_op jit(solution)/shard_map/ppermute | solution.py:249
  77.9 128.2 %all-to-all-start.1 = ((f32[16,8,64,256]{3,2,1,0:T(8,128)}), f32[16,8,64,256]{3,2,1,0:T(8,128)}, u32[]{:S(2)}, u32[]{:S(2)}) async-start(f32[16,8,64,256]{3,2,1,0:T(8,128)} %bitcast.51), calls=%async_computation.1 | async-start | bytes 16777216 | tf_op jit(solution)/shard_map/all_to_all | solution.py:254
  88.2 12.4 %copy-start.2 = (f32[2,30,64,128]{3,2,1,0:T(8,128)}, f32[2,30,64,128]{3,2,1,0:T(8,128)S(1)}, u32[]{:S(2)}) copy-start(f32[2,30,64,128]{3,2,1,0:T(8,128)S(1)} %pad_maximum_fusion.refs_0_.refs_1_) | copy-start | bytes 5898244
  88.2 45.9 %collective-permute-start.2 = (f32[2,30,64,128]{3,2,1,0:T(8,128)S(1)}, f32[2,30,64,128]{3,2,1,0:T(8,128)}, u32[]{:S(2)}, u32[]{:S(2)}) collective-permute-start(f32[2,30,64,128]{3,2,1,0:T(8,128)S(1)} %pad_maximum_fusion.refs_0_.refs_1_), channel_id=1, source_target_pairs={{0,3},{1,0},{2,1},{3,2},{4,7},{5,4},{6,5},{7,6},{8,11},{9,8},{10,9... | collective-permute-start | bytes 5898248 | tf_op jit(solution)/shard_map/ppermute | solution.py:280
  92.0 47.9 %collective-permute-start.3 = (f32[2,30,64,128]{3,2,1,0:T(8,128)S(1)}, f32[2,30,64,128]{3,2,1,0:T(8,128)}, u32[]{:S(2)}, u32[]{:S(2)}) collective-permute-start(f32[2,30,64,128]{3,2,1,0:T(8,128)S(1)} %pad_maximum_fusion.refs_0_.refs_1_), channel_id=1, source_target_pairs={{0,1},{1,2},{2,3},{3,0},{4,5},{5,6},{6,7},{7,4},{8,9},{9,10},{10,1... | collective-permute-start | bytes 5898248 | tf_op jit(solution)/shard_map/ppermute | solution.py:280
  95.6 66.7 %collective-permute-start.5 = (f32[2,20,64,128]{3,2,1,0:T(8,128)}, f32[2,20,64,128]{3,2,1,0:T(8,128)}, u32[]{:S(2)}, u32[]{:S(2)}) collective-permute-start(f32[2,20,64,128]{3,2,1,0:T(8,128)} %pad_maximum_fusion.1.refs_0_.refs_1_), channel_id=1, source_target_pairs={{0,3},{1,0},{2,1},{3,2},{4,7},{5,4},{6,5},{7,6},{8,11},{9,8},{10,9... | collective-permute-start | bytes 3932168 | tf_op jit(solution)/shard_map/ppermute | solution.py:280
  106.0 14.9 %copy-start.4 = (f32[512,512]{0,1:T(8,128)}, f32[512,512]{0,1:T(8,128)S(1)}, u32[]{:S(2)}) copy-start(f32[512,512]{0,1:T(8,128)S(1)} %copy.36) | copy-start | bytes 3145732
  109.3 58.4 %collective-permute-start.1 = (f32[2,20,64,128]{3,2,1,0:T(8,128)}, f32[2,20,64,128]{3,2,1,0:T(8,128)}, u32[]{:S(2)}, u32[]{:S(2)}) collective-permute-start(f32[2,20,64,128]{3,2,1,0:T(8,128)} %pad_maximum_fusion.1.refs_0_.refs_1_), channel_id=1, source_target_pairs={{0,1},{1,2},{2,3},{3,0},{4,5},{5,6},{6,7},{7,4},{8,9},{9,10},{10,1... | collective-permute-start | bytes 3932168 | tf_op jit(solution)/shard_map/ppermute | solution.py:280
  136.4 47.0 %collective-permute-start.8 = (f32[1,30,64,128]{3,2,1,0:T(8,128)}, f32[1,30,64,128]{3,2,1,0:T(8,128)S(1)}, u32[]{:S(2)}, u32[]{:S(2)}) collective-permute-start(f32[1,30,64,128]{3,2,1,0:T(8,128)} %slice_add_fusion), channel_id=1, source_target_pairs={{0,3},{1,0},{2,1},{3,2},{4,7},{5,4},{6,5},{7,6},{8,11},{9,8},{10,9... | collective-permute-start | bytes 2949128 | tf_op jit(solution)/shard_map/ppermute | solution.py:276
  141.1 45.2 %collective-permute-start.7 = (f32[1,30,64,128]{3,2,1,0:T(8,128)S(1)}, f32[1,30,64,128]{3,2,1,0:T(8,128)S(1)}, u32[]{:S(2)}, u32[]{:S(2)}) collective-permute-start(f32[1,30,64,128]{3,2,1,0:T(8,128)S(1)} %slice_add_fusion.1), channel_id=1, source_target_pairs={{0,1},{1,2},{2,3},{3,0},{4,5},{5,6},{6,7},{7,4},{8,9},{9,10},{10,1... | collective-permute-start | bytes 2949128 | tf_op jit(solution)/shard_map/ppermute | solution.py:275
  164.3 33.1 %collective-permute-start.6 = (f32[1,20,64,128]{3,2,1,0:T(8,128)}, f32[1,20,64,128]{3,2,1,0:T(8,128)}, u32[]{:S(2)}, u32[]{:S(2)}) collective-permute-start(f32[1,20,64,128]{3,2,1,0:T(8,128)} %slice_add_fusion.2), channel_id=1, source_target_pairs={{0,3},{1,0},{2,1},{3,2},{4,7},{5,4},{6,5},{7,6},{8,11},{9,8},{10,9... | collective-permute-start | bytes 1966088 | tf_op jit(solution)/shard_map/ppermute | solution.py:276
  169.7 30.8 %collective-permute-start.4 = (f32[1,20,64,128]{3,2,1,0:T(8,128)}, f32[1,20,64,128]{3,2,1,0:T(8,128)}, u32[]{:S(2)}, u32[]{:S(2)}) collective-permute-start(f32[1,20,64,128]{3,2,1,0:T(8,128)} %slice_add_fusion.3), channel_id=1, source_target_pairs={{0,1},{1,2},{2,3},{3,0},{4,5},{5,6},{6,7},{7,4},{8,9},{9,10},{10,1... | collective-permute-start | bytes 1966088 | tf_op jit(solution)/shard_map/ppermute | solution.py:275
  183.3 3.0 %copy-start.5 = (f32[1,30,64,128]{3,2,1,0:T(8,128)}, f32[1,30,64,128]{3,2,1,0:T(8,128)S(1)}, u32[]{:S(2)}) copy-start(f32[1,30,64,128]{3,2,1,0:T(8,128)S(1)} %collective-permute-done.8.refs_1_) | copy-start | bytes 2949124
  217.8 2.1 collective-permute-start.9
  220.9 6.3 %collective-permute-start.10 = (f32[128,256]{1,0:T(8,128)S(1)}, f32[128,256]{1,0:T(8,128)S(1)}, u32[]{:S(2)}, u32[]{:S(2)}) collective-permute-start(f32[128,256]{1,0:T(8,128)S(1)} %constant_dynamic-slice_fusion), channel_id=1, source_target_pairs={{0,64},{8,72},{16,80},{24,88},{32,96},{40,104},{48,112},{56,120},{... | collective-permute-start | bytes 393224 | tf_op jit(solution)/shard_map/ppermute | solution.py:224
  227.2 13.7 %collective-permute-start.11 = (f32[128,256]{1,0:T(8,128)S(1)}, f32[128,256]{1,0:T(8,128)S(1)}, u32[]{:S(2)}, u32[]{:S(2)}) collective-permute-start(f32[128,256]{1,0:T(8,128)S(1)} %dynamic-slice_add_fusion.1), channel_id=1, source_target_pairs={{0,16},{8,24},{16,32},{24,40},{32,48},{40,56},{48,0},{56,8},{64,80... | collective-permute-start | bytes 393224 | tf_op jit(solution)/shard_map/ppermute | solution.py:232
  234.6 10.1 %collective-permute-start.12 = (f32[128,256]{1,0:T(8,128)S(1)}, f32[128,256]{1,0:T(8,128)S(1)}, u32[]{:S(2)}, u32[]{:S(2)}) collective-permute-start(f32[128,256]{1,0:T(8,128)S(1)} %dynamic-slice_add_fusion.1), channel_id=1, source_target_pairs={{0,32},{8,40},{16,48},{24,56},{32,0},{40,8},{48,16},{56,24},{64,96... | collective-permute-start | bytes 393224 | tf_op jit(solution)/shard_map/ppermute | solution.py:232
  238.9 5.7 %collective-permute-start.13 = (f32[128,256]{1,0:T(8,128)S(1)}, f32[128,256]{1,0:T(8,128)S(1)}, u32[]{:S(2)}, u32[]{:S(2)}) collective-permute-start(f32[128,256]{1,0:T(8,128)S(1)} %dynamic-slice_add_fusion.1), channel_id=1, source_target_pairs={{0,48},{8,56},{16,0},{24,8},{32,16},{40,24},{48,32},{56,40},{64,11... | collective-permute-start | bytes 393224 | tf_op jit(solution)/shard_map/ppermute | solution.py:232
  244.7 5.4 %collective-permute-start.14 = (f32[128,256]{1,0:T(8,128)S(1)}, f32[128,256]{1,0:T(8,128)S(1)}, u32[]{:S(2)}, u32[]{:S(2)}) collective-permute-start(f32[128,256]{1,0:T(8,128)S(1)} %add_add_fusion), channel_id=1, source_target_pairs={{0,64},{8,72},{16,80},{24,88},{32,96},{40,104},{48,112},{56,120},{... | collective-permute-start | bytes 393224 | tf_op jit(solution)/shard_map/ppermute | solution.py:227
  250.1 4.0 %collective-permute-start.15 = (f32[256,256]{1,0:T(8,128)S(1)}, f32[256,256]{1,0:T(8,128)S(1)}, u32[]{:S(2)}, u32[]{:S(2)}) collective-permute-start(f32[256,256]{1,0:T(8,128)S(1)} %pad_maximum_fusion.3), channel_id=1, source_target_pairs={{0,8},{8,0},{16,24},{24,16},{32,40},{40,32},{48,56},{56,48},{64,72... | collective-permute-start | bytes 786440 | tf_op jit(solution)/shard_map/ppermute | solution.py:227
  255.0 16.0 %copy-start.1 = (f32[512,512]{1,0:T(8,128)S(1)}, f32[512,512]{1,0:T(8,128)}, u32[]{:S(2)}) copy-start(f32[512,512]{1,0:T(8,128)} %param.7) | copy-start | bytes 3145732
  (1 other events, 0.9 us)

commit v3 on v2

--- a/solution.py
+++ b/solution.py
@@ -229,7 +229,9 @@
         return jnp.concatenate([first, second])
 
     value = halve(halve(value, cc, core_perm), xh, x_perm)
-    value = value + sum(lax.ppermute(value, "row", row_perm(0, dy, 0)) for dy in (1, 2, 3))
+    for flip in (1, 3):
+        pairs = [(r, r ^ (2 * flip)) for r in range(16)]
+        value = value + lax.ppermute(value, "row", pairs)
     return join(join(value, xh, x_perm), cc, core_perm)
 
 

time: 273 us -> 274 us (level)
    ppermute x3 -> x2, waiting for transfers between devices: 5.67 us -> 4.72 us  [sum_over_rows(): value = value + lax.ppermute(value, 'row', pairs)]
    ppermute x3 -> x2, starting transfers between devices: 11.7 us -> 12.6 us  [sum_over_rows(): value = value + lax.ppermute(value, 'row', pairs)]
  transfers between devices with their start and end apart: 18 -> 17, of which waited for: 15 -> 15; matrix products, arithmetic and copies ran while one was open for 13% -> 13% of each run, Pallas kernels for 16% -> 16%
where the time goes in v3:
time: 274 us; the launch traced here: 272 us
  waiting for transfers between devices  97.8 us (36%)
  Pallas kernels  75.5 us (28%)
  starting transfers between devices  53.7 us (20%)
  local copies, waits for them, and re-layouts  28.9 us (11%)
  other arithmetic  11.4 us (4%)
  between operations  4.59 us (2%)
    pallas_call x8, Pallas kernels, prepare(): pl.pallas_call(functools.partial(prepare_kernel, skip), grid_spec=pltpu.P...  44.4 us
    all_to_all x1, waiting for transfers between devices, per_device(): lax.all_to_all(cut_tiles(reflectors.T), 'row', split_axis=0, concat_axis=...  27.8 us
    ppermute x1, waiting for transfers between devices, per_device(): across = lax.ppermute(mine, 'col', col_perm(1, 0))  27.6 us
    pallas_call x1, Pallas kernels, apply(): pl.pallas_call(apply_kernel, grid_spec=pltpu.PrefetchScalarGridSpec(num_s...  16.2 us
    ppermute x2, waiting for transfers between devices, per_device(): lax.ppermute(pair, 'col', col_perm(0, 3))  14.2 us
    ppermute x2, starting transfers between devices, sum_over_rows(): value = value + lax.ppermute(value, 'row', pairs)  12.6 us
    pallas_call x1, Pallas kernels, project(): pl.pallas_call(project_kernel, grid_spec=pltpu.PrefetchScalarGridSpec(num...  10.8 us
    all_to_all x1, starting transfers between devices, per_device(): lax.all_to_all(source, 'row', split_axis=0, concat_axis=0, tiled=True)  8.76 us
  transfers between devices with their start and end apart: 17, of which 15 were waited for; matrix products, arithmetic and copies ran while one was open for 13% of the time, Pallas kernels for 16%

profile of v3, /device:TPU:1, one launch (start us, length us, event | category | flops | bytes accessed | tf_op | source)
XLA Modules:
  0.0 272.0 jit_solution(3137653924772057250)
XLA Ops:
  0.0 4.2 %cut_tiles.1 = f32[16,4,64,128]{3,2,1,0:T(8,128)} custom-call(f32[64,8192]{1,0:T(8,128)} %bitcast.58), custom_call_target="tpu_custom_call" | custom-call | tf_op jit(solution)/shard_map/cut_tiles/pallas_call | solution.py:41
  4.2 8.4 %all-to-all-start = ((f32[16,4,64,128]{3,2,1,0:T(8,128)}), f32[16,4,64,128]{3,2,1,0:T(8,128)S(1)}, u32[]{:S(2)}, u32[]{:S(2)}) async-start(f32[16,4,64,128]{3,2,1,0:T(8,128)} %cut_tiles.1), calls=%async_computation | async-start | bytes 4194304 | tf_op jit(solution)/shard_map/all_to_all | solution.py:247
  13.3 27.8 %all-to-all-done = f32[16,4,64,128]{3,2,1,0:T(8,128)S(1)} async-done(((f32[16,4,64,128]{3,2,1,0:T(8,128)}), f32[16,4,64,128]{3,2,1,0:T(8,128)S(1)}, u32[]{:S(2)}, u32[]{:S(2)}) %all-to-all-start) | async-done | bytes 2097184 | tf_op jit(solution)/shard_map/all_to_all | solution.py:247
  42.4 7.9 %copy.38 = f32[8,16,64,256]{3,2,0,1:T(8,128)} copy(f32[8,16,64,256]{3,2,1,0:T(8,128)} %bitcast.55) | data formatting | bytes 16777216 | tf_op jit(solution)/shard_map/reshape | solution.py:254
  50.2 27.6 %collective-permute-done = f32[50,64,128]{2,1,0:T(8,128)} collective-permute-done((f32[50,64,128]{2,1,0:T(8,128)S(1)}, f32[50,64,128]{2,1,0:T(8,128)}, u32[]{:S(2)}, u32[]{:S(2)}) %collective-permute-start) | collective-permute-done | bytes 1638432 | tf_op jit(solution)/shard_map/ppermute | solution.py:251
  77.9 8.8 %all-to-all-start.1 = ((f32[16,8,64,256]{3,2,1,0:T(8,128)}), f32[16,8,64,256]{3,2,1,0:T(8,128)}, u32[]{:S(2)}, u32[]{:S(2)}) async-start(f32[16,8,64,256]{3,2,1,0:T(8,128)} %bitcast.51), calls=%async_computation.1 | async-start | bytes 16777216 | tf_op jit(solution)/shard_map/all_to_all | solution.py:256
  88.2 3.8 %collective-permute-start.2 = (f32[2,30,64,128]{3,2,1,0:T(8,128)S(1)}, f32[2,30,64,128]{3,2,1,0:T(8,128)}, u32[]{:S(2)}, u32[]{:S(2)}) collective-permute-start(f32[2,30,64,128]{3,2,1,0:T(8,128)S(1)} %pad_maximum_fusion.refs_0_.refs_1_), channel_id=1, source_target_pairs={{0,3},{1,0},{2,1},{3,2},{4,7},{5,4},{6,5},{7,6},{8,11},{9,8},{10,9... | collective-permute-start | bytes 5898248 | tf_op jit(solution)/shard_map/ppermute | solution.py:282
  110.0 6.3 %prepare.8 = (bf16[512,6400]{1,0:T(8,128)(2,1)}, bf16[512,6400]{1,0:T(8,128)(2,1)}, bf16[4,8192,128]{2,1,0:T(8,128)(2,1)}, bf16[4,8192,128]{2,1,0:T(8,128)(2,1)}, f32[8,128]{1,0:T(8,128)}) custom-call(s32[6]{0:T(128)} %broadcast_add_fusion.info, f32[2,30,64,128]{3,2,1,0:T(8,128)} %copy-done.2, f32[2,30,64,128]{3,2,1,0:T(8,128)} %copy-done.2), custom_call_target="tpu_custom_call" | custom-call | flops 1000000000 | bytes 10000000 | tf_op jit(solution)/shard_map/prepare/pallas_call | solution.py:97
  116.3 4.8 %prepare.9 = (bf16[512,6400]{1,0:T(8,128)(2,1)}, bf16[512,6400]{1,0:T(8,128)(2,1)}, bf16[4,8192,128]{2,1,0:T(8,128)(2,1)}, bf16[4,8192,128]{2,1,0:T(8,128)(2,1)}, f32[8,128]{1,0:T(8,128)}) custom-call(s32[6]{0:T(128)} %broadcast_add_fusion.info, ...), custom_call_target="tpu_custom_call", output_to_operand_aliasing={{0}: (3, {}), {1}: (4, {}), {2}: (5, {}), {3}: (6, {})} | custom-call | flops 1000000000 | bytes 10000000 | tf_op jit(solution)/shard_map/prepare/pallas_call | solution.py:97
  124.6 9.5 %collective-permute-done.2.refs_0_.refs_1_ = f32[2,30,64,128]{3,2,1,0:T(8,128)} collective-permute-done((f32[2,30,64,128]{3,2,1,0:T(8,128)S(1)}, f32[2,30,64,128]{3,2,1,0:T(8,128)}, u32[]{:S(2)}, u32[]{:S(2)}) %collective-permute-start.2) | collective-permute-done | bytes 1966112 | tf_op jit(solution)/shard_map/ppermute | solution.py:282
  141.2 6.3 %prepare.10 = (bf16[512,6400]{1,0:T(8,128)(2,1)}, bf16[512,6400]{1,0:T(8,128)(2,1)}, bf16[4,8192,128]{2,1,0:T(8,128)(2,1)}, bf16[4,8192,128]{2,1,0:T(8,128)(2,1)}, f32[8,128]{1,0:T(8,128)}) custom-call(s32[6]{0:T(128)} %stack.73.info, ...), custom_call_target="tpu_custom_call", output_to_operand_aliasing={{0}: (3, {}), {1}: (4, {}), {2}: (5, {}), {3}: (6, {})} | custom-call | flops 1000000000 | bytes 10000000 | tf_op jit(solution)/shard_map/prepare/pallas_call | solution.py:97
  147.6 6.3 %prepare.11 = (bf16[512,6400]{1,0:T(8,128)(2,1)}, bf16[512,6400]{1,0:T(8,128)(2,1)}, bf16[4,8192,128]{2,1,0:T(8,128)(2,1)}, bf16[4,8192,128]{2,1,0:T(8,128)(2,1)}, f32[8,128]{1,0:T(8,128)}) custom-call(s32[6]{0:T(128)} %stack.82.info, ...), custom_call_target="tpu_custom_call", output_to_operand_aliasing={{0}: (3, {}), {1}: (4, {}), {2}: (5, {}), {3}: (6, {})} | custom-call | flops 1000000000 | bytes 10000000 | tf_op jit(solution)/shard_map/prepare/pallas_call | solution.py:97
  157.6 4.7 %collective-permute-done.5.refs_0_.refs_1_ = f32[2,20,64,128]{3,2,1,0:T(8,128)} collective-permute-done((f32[2,20,64,128]{3,2,1,0:T(8,128)}, f32[2,20,64,128]{3,2,1,0:T(8,128)}, u32[]{:S(2)}, u32[]{:S(2)}) %collective-permute-start.5) | collective-permute-done | bytes 1310752 | tf_op jit(solution)/shard_map/ppermute | solution.py:282
  170.3 4.8 %prepare.12 = (bf16[512,6400]{1,0:T(8,128)(2,1)}, bf16[512,6400]{1,0:T(8,128)(2,1)}, bf16[4,8192,128]{2,1,0:T(8,128)(2,1)}, bf16[4,8192,128]{2,1,0:T(8,128)(2,1)}, f32[8,128]{1,0:T(8,128)}) custom-call(s32[6]{0:T(128)} %stack.73.info, ...), custom_call_target="tpu_custom_call", output_to_operand_aliasing={{0}: (3, {}), {1}: (4, {}), {2}: (5, {}), {3}: (6, {})} | custom-call | flops 1000000000 | bytes 10000000 | tf_op jit(solution)/shard_map/prepare/pallas_call | solution.py:97
  175.1 4.8 %prepare.13 = (bf16[512,6400]{1,0:T(8,128)(2,1)}, bf16[512,6400]{1,0:T(8,128)(2,1)}, bf16[4,8192,128]{2,1,0:T(8,128)(2,1)}, bf16[4,8192,128]{2,1,0:T(8,128)(2,1)}, f32[8,128]{1,0:T(8,128)}) custom-call(s32[6]{0:T(128)} %stack.82.info, ...), custom_call_target="tpu_custom_call", output_to_operand_aliasing={{0}: (3, {}), {1}: (4, {}), {2}: (5, {}), {3}: (6, {})} | custom-call | flops 1000000000 | bytes 10000000 | tf_op jit(solution)/shard_map/prepare/pallas_call | solution.py:97
  187.3 6.3 %prepare.14 = (bf16[512,6400]{1,0:T(8,128)(2,1)}, bf16[512,6400]{1,0:T(8,128)(2,1)}, bf16[4,8192,128]{2,1,0:T(8,128)(2,1)}, bf16[4,8192,128]{2,1,0:T(8,128)(2,1)}, f32[8,128]{1,0:T(8,128)}) custom-call(s32[6]{0:T(128)} %stack.67.info, f32[1,30,64,128]{3,2,1,0:T(8,128)} %copy-done.6, ...), custom_call_target="tpu_custom_call", output_to_operand_aliasing={{0}: (3, {}), {1}: (4, {}), {2}: (5, {}), {3}: (6, {})} | custom-call | flops 1000000000 | bytes 10000000 | tf_op jit(solution)/shard_map/prepare/pallas_call | solution.py:97
  193.6 3.8 %collective-permute-done.6.refs_1_ = f32[1,20,64,128]{3,2,1,0:T(8,128)} collective-permute-done((f32[1,20,64,128]{3,2,1,0:T(8,128)}, f32[1,20,64,128]{3,2,1,0:T(8,128)}, u32[]{:S(2)}, u32[]{:S(2)}) %collective-permute-start.6) | collective-permute-done | bytes 655392 | tf_op jit(solution)/shard_map/ppermute | solution.py:278
  200.5 4.7 %prepare.15 = (bf16[512,6400]{1,0:T(8,128)(2,1)}, bf16[512,6400]{1,0:T(8,128)(2,1)}, bf16[4,8192,128]{2,1,0:T(8,128)(2,1)}, bf16[4,8192,128]{2,1,0:T(8,128)(2,1)}, f32[8,128]{1,0:T(8,128)}) custom-call(s32[6]{0:T(128)} %stack.67.info, ...), custom_call_target="tpu_custom_call", output_to_operand_aliasing={{0}: (3, {}), {1}: (4, {}), {2}: (5, {}), {3}: (6, {})} | custom-call | flops 1000000000 | bytes 10000000 | tf_op jit(solution)/shard_map/prepare/pallas_call | solution.py:97
  206.1 10.8 %project.1 = f32[512,256]{1,0:T(8,128)} custom-call(s32[1]{0:T(128)} %bitcast.1.info, f32[8192,256]{1,0:T(8,128)} %bitcast.6.v_ref, bf16[512,6400]{1,0:T(8,128)(2,1)} %get-tuple-element.75.high_ref, bf16[512,6400]{1,0:T(8,128)(2,1)} %get-tuple-element.76.low_ref), custom_call_target="tpu_custom_call" | custom-call | flops 5033164800 | bytes 20000000 | tf_op jit(solution)/shard_map/project/pallas_call | solution.py:136
  223.5 3.7 %collective-permute-done.10 = f32[128,256]{1,0:T(8,128)S(1)} collective-permute-done((f32[128,256]{1,0:T(8,128)S(1)}, f32[128,256]{1,0:T(8,128)S(1)}, u32[]{:S(2)}, u32[]{:S(2)}) %collective-permute-start.10) | collective-permute-done | bytes 131104 | tf_op jit(solution)/shard_map/ppermute | solution.py:224
  227.2 7.4 %collective-permute-start.11 = (f32[128,256]{1,0:T(8,128)S(1)}, f32[128,256]{1,0:T(8,128)S(1)}, u32[]{:S(2)}, u32[]{:S(2)}) collective-permute-start(f32[128,256]{1,0:T(8,128)S(1)} %dynamic-slice_add_fusion.1), channel_id=1, source_target_pairs={{0,16},{8,24},{16,0},{24,8},{32,48},{40,56},{48,32},{56,40},{64,80... | collective-permute-start | bytes 393224 | tf_op jit(solution)/shard_map/ppermute | solution.py:234
  236.9 5.3 %collective-permute-start.12 = (f32[128,256]{1,0:T(8,128)S(1)}, f32[128,256]{1,0:T(8,128)S(1)}, u32[]{:S(2)}, u32[]{:S(2)}) collective-permute-start(f32[128,256]{1,0:T(8,128)S(1)} %add.325), channel_id=1, source_target_pairs={{0,48},{8,56},{16,32},{24,40},{32,16},{40,24},{48,0},{56,8},{64,11... | collective-permute-start | bytes 393224 | tf_op jit(solution)/shard_map/ppermute | solution.py:234
  250.0 3.7 %collective-permute-start.14 = (f32[256,256]{1,0:T(8,128)S(1)}, f32[256,256]{1,0:T(8,128)S(1)}, u32[]{:S(2)}, u32[]{:S(2)}) collective-permute-start(f32[256,256]{1,0:T(8,128)S(1)} %pad_maximum_fusion.3), channel_id=1, source_target_pairs={{0,8},{8,0},{16,24},{24,16},{32,40},{40,32},{48,56},{56,48},{64,72... | collective-permute-start | bytes 786440 | tf_op jit(solution)/shard_map/ppermute | solution.py:227
  255.8 16.2 %apply.1 = f32[8192,256]{1,0:T(8,128)} custom-call(s32[1]{0:T(128)} %bitcast.1.info, f32[8192,256]{1,0:T(8,128)} %bitcast.6.v_ref, f32[512,512]{1,0:T(8,128)} %bitcast.57, f32[512,256]{1,0:T(8,128)} %pad_maximum_fusion.2.p_ref, bf16[4,8192,128]{2,1,0:T(8,128)(2,1)} %get-tuple-element.77.high_ref, bf16[4,8192,128]{2,1,0:T(8,128)(2,1)} %get-tuple-element.78.low_ref), custom_call_target="tpu_custom_call" | custom-call | flops 5033164800 | bytes 30000000 | tf_op jit(solution)/shard_map/apply/pallas_call | solution.py:186
  (78 shorter events, 69.5 us)
Async XLA Ops:
  0.0 98.2 %copy-start = (f32[512,512]{1,0:T(8,128)S(1)}, f32[512,512]{1,0:T(8,128)}, u32[]{:S(2)}) copy-start(f32[512,512]{1,0:T(8,128)} %param.7) | copy-start | bytes 3145732
  4.2 36.9 %all-to-all-start = ((f32[16,4,64,128]{3,2,1,0:T(8,128)}), f32[16,4,64,128]{3,2,1,0:T(8,128)S(1)}, u32[]{:S(2)}, u32[]{:S(2)}) async-start(f32[16,4,64,128]{3,2,1,0:T(8,128)} %cut_tiles.1), calls=%async_computation | async-start | bytes 4194304 | tf_op jit(solution)/shard_map/all_to_all | solution.py:247
  41.1 45.5 %copy-start.3 = (f32[16,4,64,128]{3,2,1,0:T(8,128)}, f32[16,4,64,128]{3,2,1,0:T(8,128)S(1)}, u32[]{:S(2)}) copy-start(f32[16,4,64,128]{3,2,1,0:T(8,128)S(1)} %all-to-all-done) | copy-start | bytes 6291460
  41.3 36.6 %collective-permute-start = (f32[50,64,128]{2,1,0:T(8,128)S(1)}, f32[50,64,128]{2,1,0:T(8,128)}, u32[]{:S(2)}, u32[]{:S(2)}) collective-permute-start(f32[50,64,128]{2,1,0:T(8,128)S(1)} %constant_dynamic-slice_fusion.2), channel_id=1, source_target_pairs={{0,4},{1,5},{2,6},{3,7},{4,0},{5,1},{6,2},{7,3},{8,12},{9,13},{10,... | collective-permute-start | bytes 4915208 | tf_op jit(solution)/shard_map/ppermute | solution.py:251
  77.9 128.2 %all-to-all-start.1 = ((f32[16,8,64,256]{3,2,1,0:T(8,128)}), f32[16,8,64,256]{3,2,1,0:T(8,128)}, u32[]{:S(2)}, u32[]{:S(2)}) async-start(f32[16,8,64,256]{3,2,1,0:T(8,128)} %bitcast.51), calls=%async_computation.1 | async-start | bytes 16777216 | tf_op jit(solution)/shard_map/all_to_all | solution.py:256
  88.2 12.4 %copy-start.2 = (f32[2,30,64,128]{3,2,1,0:T(8,128)}, f32[2,30,64,128]{3,2,1,0:T(8,128)S(1)}, u32[]{:S(2)}) copy-start(f32[2,30,64,128]{3,2,1,0:T(8,128)S(1)} %pad_maximum_fusion.refs_0_.refs_1_) | copy-start | bytes 5898244
  88.2 45.9 %collective-permute-start.2 = (f32[2,30,64,128]{3,2,1,0:T(8,128)S(1)}, f32[2,30,64,128]{3,2,1,0:T(8,128)}, u32[]{:S(2)}, u32[]{:S(2)}) collective-permute-start(f32[2,30,64,128]{3,2,1,0:T(8,128)S(1)} %pad_maximum_fusion.refs_0_.refs_1_), channel_id=1, source_target_pairs={{0,3},{1,0},{2,1},{3,2},{4,7},{5,4},{6,5},{7,6},{8,11},{9,8},{10,9... | collective-permute-start | bytes 5898248 | tf_op jit(solution)/shard_map/ppermute | solution.py:282
  92.0 47.9 %collective-permute-start.3 = (f32[2,30,64,128]{3,2,1,0:T(8,128)S(1)}, f32[2,30,64,128]{3,2,1,0:T(8,128)}, u32[]{:S(2)}, u32[]{:S(2)}) collective-permute-start(f32[2,30,64,128]{3,2,1,0:T(8,128)S(1)} %pad_maximum_fusion.refs_0_.refs_1_), channel_id=1, source_target_pairs={{0,1},{1,2},{2,3},{3,0},{4,5},{5,6},{6,7},{7,4},{8,9},{9,10},{10,1... | collective-permute-start | bytes 5898248 | tf_op jit(solution)/shard_map/ppermute | solution.py:282
  95.6 66.7 %collective-permute-start.5 = (f32[2,20,64,128]{3,2,1,0:T(8,128)}, f32[2,20,64,128]{3,2,1,0:T(8,128)}, u32[]{:S(2)}, u32[]{:S(2)}) collective-permute-start(f32[2,20,64,128]{3,2,1,0:T(8,128)} %pad_maximum_fusion.1.refs_0_.refs_1_), channel_id=1, source_target_pairs={{0,3},{1,0},{2,1},{3,2},{4,7},{5,4},{6,5},{7,6},{8,11},{9,8},{10,9... | collective-permute-start | bytes 3932168 | tf_op jit(solution)/shard_map/ppermute | solution.py:282
  106.0 15.0 %copy-start.4 = (f32[512,512]{0,1:T(8,128)}, f32[512,512]{0,1:T(8,128)S(1)}, u32[]{:S(2)}) copy-start(f32[512,512]{0,1:T(8,128)S(1)} %copy.36) | copy-start | bytes 3145732
  109.4 58.3 %collective-permute-start.1 = (f32[2,20,64,128]{3,2,1,0:T(8,128)}, f32[2,20,64,128]{3,2,1,0:T(8,128)}, u32[]{:S(2)}, u32[]{:S(2)}) collective-permute-start(f32[2,20,64,128]{3,2,1,0:T(8,128)} %pad_maximum_fusion.1.refs_0_.refs_1_), channel_id=1, source_target_pairs={{0,1},{1,2},{2,3},{3,0},{4,5},{5,6},{6,7},{7,4},{8,9},{9,10},{10,1... | collective-permute-start | bytes 3932168 | tf_op jit(solution)/shard_map/ppermute | solution.py:282
  136.3 47.0 %collective-permute-start.8 = (f32[1,30,64,128]{3,2,1,0:T(8,128)}, f32[1,30,64,128]{3,2,1,0:T(8,128)S(1)}, u32[]{:S(2)}, u32[]{:S(2)}) collective-permute-start(f32[1,30,64,128]{3,2,1,0:T(8,128)} %slice_add_fusion), channel_id=1, source_target_pairs={{0,3},{1,0},{2,1},{3,2},{4,7},{5,4},{6,5},{7,6},{8,11},{9,8},{10,9... | collective-permute-start | bytes 2949128 | tf_op jit(solution)/shard_map/ppermute | solution.py:278
  141.1 45.2 %collective-permute-start.7 = (f32[1,30,64,128]{3,2,1,0:T(8,128)S(1)}, f32[1,30,64,128]{3,2,1,0:T(8,128)S(1)}, u32[]{:S(2)}, u32[]{:S(2)}) collective-permute-start(f32[1,30,64,128]{3,2,1,0:T(8,128)S(1)} %slice_add_fusion.1), channel_id=1, source_target_pairs={{0,1},{1,2},{2,3},{3,0},{4,5},{5,6},{6,7},{7,4},{8,9},{9,10},{10,1... | collective-permute-start | bytes 2949128 | tf_op jit(solution)/shard_map/ppermute | solution.py:277
  164.3 33.1 %collective-permute-start.6 = (f32[1,20,64,128]{3,2,1,0:T(8,128)}, f32[1,20,64,128]{3,2,1,0:T(8,128)}, u32[]{:S(2)}, u32[]{:S(2)}) collective-permute-start(f32[1,20,64,128]{3,2,1,0:T(8,128)} %slice_add_fusion.2), channel_id=1, source_target_pairs={{0,3},{1,0},{2,1},{3,2},{4,7},{5,4},{6,5},{7,6},{8,11},{9,8},{10,9... | collective-permute-start | bytes 1966088 | tf_op jit(solution)/shard_map/ppermute | solution.py:278
  169.7 30.8 %collective-permute-start.4 = (f32[1,20,64,128]{3,2,1,0:T(8,128)}, f32[1,20,64,128]{3,2,1,0:T(8,128)}, u32[]{:S(2)}, u32[]{:S(2)}) collective-permute-start(f32[1,20,64,128]{3,2,1,0:T(8,128)} %slice_add_fusion.3), channel_id=1, source_target_pairs={{0,1},{1,2},{2,3},{3,0},{4,5},{5,6},{6,7},{7,4},{8,9},{9,10},{10,1... | collective-permute-start | bytes 1966088 | tf_op jit(solution)/shard_map/ppermute | solution.py:277
  183.3 3.0 %copy-start.5 = (f32[1,30,64,128]{3,2,1,0:T(8,128)}, f32[1,30,64,128]{3,2,1,0:T(8,128)S(1)}, u32[]{:S(2)}) copy-start(f32[1,30,64,128]{3,2,1,0:T(8,128)S(1)} %collective-permute-done.8.refs_1_) | copy-start | bytes 2949124
  186.3 0.9 copy-start.6
  217.8 2.1 collective-permute-start.9
  220.9 6.3 %collective-permute-start.10 = (f32[128,256]{1,0:T(8,128)S(1)}, f32[128,256]{1,0:T(8,128)S(1)}, u32[]{:S(2)}, u32[]{:S(2)}) collective-permute-start(f32[128,256]{1,0:T(8,128)S(1)} %constant_dynamic-slice_fusion), channel_id=1, source_target_pairs={{0,64},{8,72},{16,80},{24,88},{32,96},{40,104},{48,112},{56,120},{... | collective-permute-start | bytes 393224 | tf_op jit(solution)/shard_map/ppermute | solution.py:224
  227.2 9.7 %collective-permute-start.11 = (f32[128,256]{1,0:T(8,128)S(1)}, f32[128,256]{1,0:T(8,128)S(1)}, u32[]{:S(2)}, u32[]{:S(2)}) collective-permute-start(f32[128,256]{1,0:T(8,128)S(1)} %dynamic-slice_add_fusion.1), channel_id=1, source_target_pairs={{0,16},{8,24},{16,0},{24,8},{32,48},{40,56},{48,32},{56,40},{64,80... | collective-permute-start | bytes 393224 | tf_op jit(solution)/shard_map/ppermute | solution.py:234
  236.9 7.6 %collective-permute-start.12 = (f32[128,256]{1,0:T(8,128)S(1)}, f32[128,256]{1,0:T(8,128)S(1)}, u32[]{:S(2)}, u32[]{:S(2)}) collective-permute-start(f32[128,256]{1,0:T(8,128)S(1)} %add.325), channel_id=1, source_target_pairs={{0,48},{8,56},{16,32},{24,40},{32,16},{40,24},{48,0},{56,8},{64,11... | collective-permute-start | bytes 393224 | tf_op jit(solution)/shard_map/ppermute | solution.py:234
  244.6 5.4 %collective-permute-start.13 = (f32[128,256]{1,0:T(8,128)S(1)}, f32[128,256]{1,0:T(8,128)S(1)}, u32[]{:S(2)}, u32[]{:S(2)}) collective-permute-start(f32[128,256]{1,0:T(8,128)S(1)} %add.326), channel_id=1, source_target_pairs={{0,64},{8,72},{16,80},{24,88},{32,96},{40,104},{48,112},{56,120},{... | collective-permute-start | bytes 393224 | tf_op jit(solution)/shard_map/ppermute | solution.py:227
  250.0 4.8 %collective-permute-start.14 = (f32[256,256]{1,0:T(8,128)S(1)}, f32[256,256]{1,0:T(8,128)S(1)}, u32[]{:S(2)}, u32[]{:S(2)}) collective-permute-start(f32[256,256]{1,0:T(8,128)S(1)} %pad_maximum_fusion.3), channel_id=1, source_target_pairs={{0,8},{8,0},{16,24},{24,16},{32,40},{40,32},{48,56},{56,48},{64,72... | collective-permute-start | bytes 786440 | tf_op jit(solution)/shard_map/ppermute | solution.py:227
  255.8 16.2 %copy-start.1 = (f32[512,512]{1,0:T(8,128)S(1)}, f32[512,512]{1,0:T(8,128)}, u32[]{:S(2)}) copy-start(f32[512,512]{1,0:T(8,128)} %param.7) | copy-start | bytes 3145732

commit v4 on v2

--- a/solution.py
+++ b/solution.py
@@ -127,7 +127,7 @@
 
 def project(info, cyc_v, high, low):
     width, count = cyc_v.shape[1], high.shape[0]
-    rows = 2 * STEP * BLOCK
+    rows = 5 * STEP * BLOCK
     wide = pl.BlockSpec((count, rows), lambda i, s: (0, i))
     window = pl.BlockSpec(
         (pl.Element(rows), pl.Element(width)),
@@ -179,7 +179,7 @@
 
 def apply(info, cyc_v, t_rel, products, high, low):
     nb, (height, width) = high.shape[0] * BLOCK, cyc_v.shape
-    rows = 8 * BLOCK
+    rows = 16 * BLOCK
     held = lambda i, s: jnp.clip(i, s[0] * BLOCK // rows, (s[0] * BLOCK + SPAN - 1) // rows)
     tall = pl.BlockSpec((nb // BLOCK, rows, BLOCK), lambda i, s: (0, held(i, s), 0))
     plain = pl.BlockSpec((rows, width), lambda i, s: (i, 0))

time: 273 us -> 272 us (level)
  no operation moved by 1% of the time
where the time goes in v4:
time: 272 us; the launch traced here: 270 us
  waiting for transfers between devices  98.5 us (36%)
  Pallas kernels  73.9 us (27%)
  starting transfers between devices  52.3 us (19%)
  local copies, waits for them, and re-layouts  29.1 us (11%)
  other arithmetic  11.4 us (4%)
  between operations  4.67 us (2%)
    pallas_call x8, Pallas kernels, prepare(): pl.pallas_call(functools.partial(prepare_kernel, skip), grid_spec=pltpu.P...  44.3 us
    all_to_all x1, waiting for transfers between devices, per_device(): lax.all_to_all(cut_tiles(reflectors.T), 'row', split_axis=0, concat_axis=...  27.8 us
    ppermute x1, waiting for transfers between devices, per_device(): across = lax.ppermute(mine, 'col', col_perm(1, 0))  27.6 us
    pallas_call x1, Pallas kernels, apply(): pl.pallas_call(apply_kernel, grid_spec=pltpu.PrefetchScalarGridSpec(num_s...  15.2 us
    ppermute x2, waiting for transfers between devices, per_device(): lax.ppermute(pair, 'col', col_perm(0, 3))  14 us
    ppermute x3, starting transfers between devices, sum_over_rows(): lax.ppermute(value, 'row', row_perm(0, dy, 0))  11.7 us
    pallas_call x1, Pallas kernels, project(): pl.pallas_call(project_kernel, grid_spec=pltpu.PrefetchScalarGridSpec(num...  10.2 us
    all_to_all x1, starting transfers between devices, per_device(): lax.all_to_all(source, 'row', split_axis=0, concat_axis=0, tiled=True)  8.76 us
  transfers between devices with their start and end apart: 18, of which 15 were waited for; matrix products, arithmetic and copies ran while one was open for 13% of the time, Pallas kernels for 16%

profile of v4, /device:TPU:1, one launch (start us, length us, event | category | flops | bytes accessed | tf_op | source)
XLA Modules:
  0.0 269.8 jit_solution(8401282458611628348)
XLA Ops:
  0.0 4.2 %cut_tiles.1 = f32[16,4,64,128]{3,2,1,0:T(8,128)} custom-call(f32[64,8192]{1,0:T(8,128)} %bitcast.58), custom_call_target="tpu_custom_call" | custom-call | tf_op jit(solution)/shard_map/cut_tiles/pallas_call | solution.py:41
  4.2 8.4 %all-to-all-start = ((f32[16,4,64,128]{3,2,1,0:T(8,128)}), f32[16,4,64,128]{3,2,1,0:T(8,128)S(1)}, u32[]{:S(2)}, u32[]{:S(2)}) async-start(f32[16,4,64,128]{3,2,1,0:T(8,128)} %cut_tiles.1), calls=%async_computation | async-start | bytes 4194304 | tf_op jit(solution)/shard_map/all_to_all | solution.py:245
  13.3 27.8 %all-to-all-done = f32[16,4,64,128]{3,2,1,0:T(8,128)S(1)} async-done(((f32[16,4,64,128]{3,2,1,0:T(8,128)}), f32[16,4,64,128]{3,2,1,0:T(8,128)S(1)}, u32[]{:S(2)}, u32[]{:S(2)}) %all-to-all-start) | async-done | bytes 2097184 | tf_op jit(solution)/shard_map/all_to_all | solution.py:245
  42.4 7.9 %copy.38 = f32[8,16,64,256]{3,2,0,1:T(8,128)} copy(f32[8,16,64,256]{3,2,1,0:T(8,128)} %bitcast.55) | data formatting | bytes 16777216 | tf_op jit(solution)/shard_map/reshape | solution.py:252
  50.2 27.6 %collective-permute-done = f32[50,64,128]{2,1,0:T(8,128)} collective-permute-done((f32[50,64,128]{2,1,0:T(8,128)S(1)}, f32[50,64,128]{2,1,0:T(8,128)}, u32[]{:S(2)}, u32[]{:S(2)}) %collective-permute-start) | collective-permute-done | bytes 1638432 | tf_op jit(solution)/shard_map/ppermute | solution.py:249
  77.9 8.8 %all-to-all-start.1 = ((f32[16,8,64,256]{3,2,1,0:T(8,128)}), f32[16,8,64,256]{3,2,1,0:T(8,128)}, u32[]{:S(2)}, u32[]{:S(2)}) async-start(f32[16,8,64,256]{3,2,1,0:T(8,128)} %bitcast.51), calls=%async_computation.1 | async-start | bytes 16777216 | tf_op jit(solution)/shard_map/all_to_all | solution.py:254
  88.2 3.8 %collective-permute-start.2 = (f32[2,30,64,128]{3,2,1,0:T(8,128)S(1)}, f32[2,30,64,128]{3,2,1,0:T(8,128)}, u32[]{:S(2)}, u32[]{:S(2)}) collective-permute-start(f32[2,30,64,128]{3,2,1,0:T(8,128)S(1)} %pad_maximum_fusion.refs_0_.refs_1_), channel_id=1, source_target_pairs={{0,3},{1,0},{2,1},{3,2},{4,7},{5,4},{6,5},{7,6},{8,11},{9,8},{10,9... | collective-permute-start | bytes 5898248 | tf_op jit(solution)/shard_map/ppermute | solution.py:280
  109.8 6.3 %prepare.8 = (bf16[512,6400]{1,0:T(8,128)(2,1)}, bf16[512,6400]{1,0:T(8,128)(2,1)}, bf16[4,8192,128]{2,1,0:T(8,128)(2,1)}, bf16[4,8192,128]{2,1,0:T(8,128)(2,1)}, f32[8,128]{1,0:T(8,128)}) custom-call(s32[6]{0:T(128)} %broadcast_add_fusion.info, f32[2,30,64,128]{3,2,1,0:T(8,128)} %copy-done.2, f32[2,30,64,128]{3,2,1,0:T(8,128)} %copy-done.2), custom_call_target="tpu_custom_call" | custom-call | flops 1000000000 | bytes 10000000 | tf_op jit(solution)/shard_map/prepare/pallas_call | solution.py:97
  116.1 4.7 %prepare.9 = (bf16[512,6400]{1,0:T(8,128)(2,1)}, bf16[512,6400]{1,0:T(8,128)(2,1)}, bf16[4,8192,128]{2,1,0:T(8,128)(2,1)}, bf16[4,8192,128]{2,1,0:T(8,128)(2,1)}, f32[8,128]{1,0:T(8,128)}) custom-call(s32[6]{0:T(128)} %broadcast_add_fusion.info, ...), custom_call_target="tpu_custom_call", output_to_operand_aliasing={{0}: (3, {}), {1}: (4, {}), {2}: (5, {}), {3}: (6, {})} | custom-call | flops 1000000000 | bytes 10000000 | tf_op jit(solution)/shard_map/prepare/pallas_call | solution.py:97
  124.6 9.4 %collective-permute-done.2.refs_0_.refs_1_ = f32[2,30,64,128]{3,2,1,0:T(8,128)} collective-permute-done((f32[2,30,64,128]{3,2,1,0:T(8,128)S(1)}, f32[2,30,64,128]{3,2,1,0:T(8,128)}, u32[]{:S(2)}, u32[]{:S(2)}) %collective-permute-start.2) | collective-permute-done | bytes 1966112 | tf_op jit(solution)/shard_map/ppermute | solution.py:280
  141.2 6.3 %prepare.10 = (bf16[512,6400]{1,0:T(8,128)(2,1)}, bf16[512,6400]{1,0:T(8,128)(2,1)}, bf16[4,8192,128]{2,1,0:T(8,128)(2,1)}, bf16[4,8192,128]{2,1,0:T(8,128)(2,1)}, f32[8,128]{1,0:T(8,128)}) custom-call(s32[6]{0:T(128)} %stack.73.info, ...), custom_call_target="tpu_custom_call", output_to_operand_aliasing={{0}: (3, {}), {1}: (4, {}), {2}: (5, {}), {3}: (6, {})} | custom-call | flops 1000000000 | bytes 10000000 | tf_op jit(solution)/shard_map/prepare/pallas_call | solution.py:97
  147.6 6.4 %prepare.11 = (bf16[512,6400]{1,0:T(8,128)(2,1)}, bf16[512,6400]{1,0:T(8,128)(2,1)}, bf16[4,8192,128]{2,1,0:T(8,128)(2,1)}, bf16[4,8192,128]{2,1,0:T(8,128)(2,1)}, f32[8,128]{1,0:T(8,128)}) custom-call(s32[6]{0:T(128)} %stack.82.info, ...), custom_call_target="tpu_custom_call", output_to_operand_aliasing={{0}: (3, {}), {1}: (4, {}), {2}: (5, {}), {3}: (6, {})} | custom-call | flops 1000000000 | bytes 10000000 | tf_op jit(solution)/shard_map/prepare/pallas_call | solution.py:97
  157.7 4.6 %collective-permute-done.5.refs_0_.refs_1_ = f32[2,20,64,128]{3,2,1,0:T(8,128)} collective-permute-done((f32[2,20,64,128]{3,2,1,0:T(8,128)}, f32[2,20,64,128]{3,2,1,0:T(8,128)}, u32[]{:S(2)}, u32[]{:S(2)}) %collective-permute-start.5) | collective-permute-done | bytes 1310752 | tf_op jit(solution)/shard_map/ppermute | solution.py:280
  170.3 4.8 %prepare.12 = (bf16[512,6400]{1,0:T(8,128)(2,1)}, bf16[512,6400]{1,0:T(8,128)(2,1)}, bf16[4,8192,128]{2,1,0:T(8,128)(2,1)}, bf16[4,8192,128]{2,1,0:T(8,128)(2,1)}, f32[8,128]{1,0:T(8,128)}) custom-call(s32[6]{0:T(128)} %stack.73.info, ...), custom_call_target="tpu_custom_call", output_to_operand_aliasing={{0}: (3, {}), {1}: (4, {}), {2}: (5, {}), {3}: (6, {})} | custom-call | flops 1000000000 | bytes 10000000 | tf_op jit(solution)/shard_map/prepare/pallas_call | solution.py:97
  175.1 4.7 %prepare.13 = (bf16[512,6400]{1,0:T(8,128)(2,1)}, bf16[512,6400]{1,0:T(8,128)(2,1)}, bf16[4,8192,128]{2,1,0:T(8,128)(2,1)}, bf16[4,8192,128]{2,1,0:T(8,128)(2,1)}, f32[8,128]{1,0:T(8,128)}) custom-call(s32[6]{0:T(128)} %stack.82.info, ...), custom_call_target="tpu_custom_call", output_to_operand_aliasing={{0}: (3, {}), {1}: (4, {}), {2}: (5, {}), {3}: (6, {})} | custom-call | flops 1000000000 | bytes 10000000 | tf_op jit(solution)/shard_map/prepare/pallas_call | solution.py:97
  187.2 6.3 %prepare.14 = (bf16[512,6400]{1,0:T(8,128)(2,1)}, bf16[512,6400]{1,0:T(8,128)(2,1)}, bf16[4,8192,128]{2,1,0:T(8,128)(2,1)}, bf16[4,8192,128]{2,1,0:T(8,128)(2,1)}, f32[8,128]{1,0:T(8,128)}) custom-call(s32[6]{0:T(128)} %stack.67.info, f32[1,30,64,128]{3,2,1,0:T(8,128)} %copy-done.6, ...), custom_call_target="tpu_custom_call", output_to_operand_aliasing={{0}: (3, {}), {1}: (4, {}), {2}: (5, {}), {3}: (6, {})} | custom-call | flops 1000000000 | bytes 10000000 | tf_op jit(solution)/shard_map/prepare/pallas_call | solution.py:97
  193.6 3.8 %collective-permute-done.6.refs_1_ = f32[1,20,64,128]{3,2,1,0:T(8,128)} collective-permute-done((f32[1,20,64,128]{3,2,1,0:T(8,128)}, f32[1,20,64,128]{3,2,1,0:T(8,128)}, u32[]{:S(2)}, u32[]{:S(2)}) %collective-permute-start.6) | collective-permute-done | bytes 655392 | tf_op jit(solution)/shard_map/ppermute | solution.py:276
  200.5 4.8 %prepare.15 = (bf16[512,6400]{1,0:T(8,128)(2,1)}, bf16[512,6400]{1,0:T(8,128)(2,1)}, bf16[4,8192,128]{2,1,0:T(8,128)(2,1)}, bf16[4,8192,128]{2,1,0:T(8,128)(2,1)}, f32[8,128]{1,0:T(8,128)}) custom-call(s32[6]{0:T(128)} %stack.67.info, ...), custom_call_target="tpu_custom_call", output_to_operand_aliasing={{0}: (3, {}), {1}: (4, {}), {2}: (5, {}), {3}: (6, {})} | custom-call | flops 1000000000 | bytes 10000000 | tf_op jit(solution)/shard_map/prepare/pallas_call | solution.py:97
  206.1 10.2 %project.1 = f32[512,256]{1,0:T(8,128)} custom-call(s32[1]{0:T(128)} %bitcast.1.info, f32[8192,256]{1,0:T(8,128)} %bitcast.6.v_ref, bf16[512,6400]{1,0:T(8,128)(2,1)} %get-tuple-element.75.high_ref, bf16[512,6400]{1,0:T(8,128)(2,1)} %get-tuple-element.76.low_ref), custom_call_target="tpu_custom_call" | custom-call | flops 5033164800 | bytes 20000000 | tf_op jit(solution)/shard_map/project/pallas_call | solution.py:136
  223.1 3.7 %collective-permute-done.10 = f32[128,256]{1,0:T(8,128)S(1)} collective-permute-done((f32[128,256]{1,0:T(8,128)S(1)}, f32[128,256]{1,0:T(8,128)S(1)}, u32[]{:S(2)}, u32[]{:S(2)}) %collective-permute-start.10) | collective-permute-done | bytes 131104 | tf_op jit(solution)/shard_map/ppermute | solution.py:224
  226.8 7.3 %collective-permute-start.11 = (f32[128,256]{1,0:T(8,128)S(1)}, f32[128,256]{1,0:T(8,128)S(1)}, u32[]{:S(2)}, u32[]{:S(2)}) collective-permute-start(f32[128,256]{1,0:T(8,128)S(1)} %dynamic-slice_add_fusion.1), channel_id=1, source_target_pairs={{0,16},{8,24},{16,32},{24,40},{32,48},{40,56},{48,0},{56,8},{64,80... | collective-permute-start | bytes 393224 | tf_op jit(solution)/shard_map/ppermute | solution.py:232
  234.2 4.4 %collective-permute-start.12 = (f32[128,256]{1,0:T(8,128)S(1)}, f32[128,256]{1,0:T(8,128)S(1)}, u32[]{:S(2)}, u32[]{:S(2)}) collective-permute-start(f32[128,256]{1,0:T(8,128)S(1)} %dynamic-slice_add_fusion.1), channel_id=1, source_target_pairs={{0,32},{8,40},{16,48},{24,56},{32,0},{40,8},{48,16},{56,24},{64,96... | collective-permute-start | bytes 393224 | tf_op jit(solution)/shard_map/ppermute | solution.py:232
  240.5 3.7 %collective-permute-done.12 = f32[128,256]{1,0:T(8,128)S(1)} collective-permute-done((f32[128,256]{1,0:T(8,128)S(1)}, f32[128,256]{1,0:T(8,128)S(1)}, u32[]{:S(2)}, u32[]{:S(2)}) %collective-permute-start.12) | collective-permute-done | bytes 131104 | tf_op jit(solution)/shard_map/ppermute | solution.py:232
  254.6 15.2 %apply.1 = f32[8192,256]{1,0:T(8,128)} custom-call(s32[1]{0:T(128)} %bitcast.1.info, f32[8192,256]{1,0:T(8,128)} %bitcast.6.v_ref, f32[512,512]{1,0:T(8,128)} %bitcast.57, f32[512,256]{1,0:T(8,128)} %pad_maximum_fusion.2.p_ref, bf16[4,8192,128]{2,1,0:T(8,128)(2,1)} %get-tuple-element.77.high_ref, bf16[4,8192,128]{2,1,0:T(8,128)(2,1)} %get-tuple-element.78.low_ref), custom_call_target="tpu_custom_call" | custom-call | flops 5033164800 | bytes 30000000 | tf_op jit(solution)/shard_map/apply/pallas_call | solution.py:186
  (79 shorter events, 70.0 us)
Async XLA Ops:
  0.0 98.2 %copy-start = (f32[512,512]{1,0:T(8,128)S(1)}, f32[512,512]{1,0:T(8,128)}, u32[]{:S(2)}) copy-start(f32[512,512]{1,0:T(8,128)} %param.7) | copy-start | bytes 3145732
  4.2 36.9 %all-to-all-start = ((f32[16,4,64,128]{3,2,1,0:T(8,128)}), f32[16,4,64,128]{3,2,1,0:T(8,128)S(1)}, u32[]{:S(2)}, u32[]{:S(2)}) async-start(f32[16,4,64,128]{3,2,1,0:T(8,128)} %cut_tiles.1), calls=%async_computation | async-start | bytes 4194304 | tf_op jit(solution)/shard_map/all_to_all | solution.py:245
  41.1 45.5 %copy-start.3 = (f32[16,4,64,128]{3,2,1,0:T(8,128)}, f32[16,4,64,128]{3,2,1,0:T(8,128)S(1)}, u32[]{:S(2)}) copy-start(f32[16,4,64,128]{3,2,1,0:T(8,128)S(1)} %all-to-all-done) | copy-start | bytes 6291460
  41.3 36.6 %collective-permute-start = (f32[50,64,128]{2,1,0:T(8,128)S(1)}, f32[50,64,128]{2,1,0:T(8,128)}, u32[]{:S(2)}, u32[]{:S(2)}) collective-permute-start(f32[50,64,128]{2,1,0:T(8,128)S(1)} %constant_dynamic-slice_fusion.2), channel_id=1, source_target_pairs={{0,4},{1,5},{2,6},{3,7},{4,0},{5,1},{6,2},{7,3},{8,12},{9,13},{10,... | collective-permute-start | bytes 4915208 | tf_op jit(solution)/shard_map/ppermute | solution.py:249
  77.9 128.2 %all-to-all-start.1 = ((f32[16,8,64,256]{3,2,1,0:T(8,128)}), f32[16,8,64,256]{3,2,1,0:T(8,128)}, u32[]{:S(2)}, u32[]{:S(2)}) async-start(f32[16,8,64,256]{3,2,1,0:T(8,128)} %bitcast.51), calls=%async_computation.1 | async-start | bytes 16777216 | tf_op jit(solution)/shard_map/all_to_all | solution.py:254
  88.2 12.4 %copy-start.2 = (f32[2,30,64,128]{3,2,1,0:T(8,128)}, f32[2,30,64,128]{3,2,1,0:T(8,128)S(1)}, u32[]{:S(2)}) copy-start(f32[2,30,64,128]{3,2,1,0:T(8,128)S(1)} %pad_maximum_fusion.refs_0_.refs_1_) | copy-start | bytes 5898244
  88.2 45.9 %collective-permute-start.2 = (f32[2,30,64,128]{3,2,1,0:T(8,128)S(1)}, f32[2,30,64,128]{3,2,1,0:T(8,128)}, u32[]{:S(2)}, u32[]{:S(2)}) collective-permute-start(f32[2,30,64,128]{3,2,1,0:T(8,128)S(1)} %pad_maximum_fusion.refs_0_.refs_1_), channel_id=1, source_target_pairs={{0,3},{1,0},{2,1},{3,2},{4,7},{5,4},{6,5},{7,6},{8,11},{9,8},{10,9... | collective-permute-start | bytes 5898248 | tf_op jit(solution)/shard_map/ppermute | solution.py:280
  92.0 47.9 %collective-permute-start.3 = (f32[2,30,64,128]{3,2,1,0:T(8,128)S(1)}, f32[2,30,64,128]{3,2,1,0:T(8,128)}, u32[]{:S(2)}, u32[]{:S(2)}) collective-permute-start(f32[2,30,64,128]{3,2,1,0:T(8,128)S(1)} %pad_maximum_fusion.refs_0_.refs_1_), channel_id=1, source_target_pairs={{0,1},{1,2},{2,3},{3,0},{4,5},{5,6},{6,7},{7,4},{8,9},{9,10},{10,1... | collective-permute-start | bytes 5898248 | tf_op jit(solution)/shard_map/ppermute | solution.py:280
  95.6 66.7 %collective-permute-start.5 = (f32[2,20,64,128]{3,2,1,0:T(8,128)}, f32[2,20,64,128]{3,2,1,0:T(8,128)}, u32[]{:S(2)}, u32[]{:S(2)}) collective-permute-start(f32[2,20,64,128]{3,2,1,0:T(8,128)} %pad_maximum_fusion.1.refs_0_.refs_1_), channel_id=1, source_target_pairs={{0,3},{1,0},{2,1},{3,2},{4,7},{5,4},{6,5},{7,6},{8,11},{9,8},{10,9... | collective-permute-start | bytes 3932168 | tf_op jit(solution)/shard_map/ppermute | solution.py:280
  106.0 14.8 %copy-start.4 = (f32[512,512]{0,1:T(8,128)}, f32[512,512]{0,1:T(8,128)S(1)}, u32[]{:S(2)}) copy-start(f32[512,512]{0,1:T(8,128)S(1)} %copy.36) | copy-start | bytes 3145732
  109.3 58.4 %collective-permute-start.1 = (f32[2,20,64,128]{3,2,1,0:T(8,128)}, f32[2,20,64,128]{3,2,1,0:T(8,128)}, u32[]{:S(2)}, u32[]{:S(2)}) collective-permute-start(f32[2,20,64,128]{3,2,1,0:T(8,128)} %pad_maximum_fusion.1.refs_0_.refs_1_), channel_id=1, source_target_pairs={{0,1},{1,2},{2,3},{3,0},{4,5},{5,6},{6,7},{7,4},{8,9},{9,10},{10,1... | collective-permute-start | bytes 3932168 | tf_op jit(solution)/shard_map/ppermute | solution.py:280
  136.4 47.0 %collective-permute-start.8 = (f32[1,30,64,128]{3,2,1,0:T(8,128)}, f32[1,30,64,128]{3,2,1,0:T(8,128)S(1)}, u32[]{:S(2)}, u32[]{:S(2)}) collective-permute-start(f32[1,30,64,128]{3,2,1,0:T(8,128)} %slice_add_fusion), channel_id=1, source_target_pairs={{0,3},{1,0},{2,1},{3,2},{4,7},{5,4},{6,5},{7,6},{8,11},{9,8},{10,9... | collective-permute-start | bytes 2949128 | tf_op jit(solution)/shard_map/ppermute | solution.py:276
  141.1 45.2 %collective-permute-start.7 = (f32[1,30,64,128]{3,2,1,0:T(8,128)S(1)}, f32[1,30,64,128]{3,2,1,0:T(8,128)S(1)}, u32[]{:S(2)}, u32[]{:S(2)}) collective-permute-start(f32[1,30,64,128]{3,2,1,0:T(8,128)S(1)} %slice_add_fusion.1), channel_id=1, source_target_pairs={{0,1},{1,2},{2,3},{3,0},{4,5},{5,6},{6,7},{7,4},{8,9},{9,10},{10,1... | collective-permute-start | bytes 2949128 | tf_op jit(solution)/shard_map/ppermute | solution.py:275
  164.3 33.1 %collective-permute-start.6 = (f32[1,20,64,128]{3,2,1,0:T(8,128)}, f32[1,20,64,128]{3,2,1,0:T(8,128)}, u32[]{:S(2)}, u32[]{:S(2)}) collective-permute-start(f32[1,20,64,128]{3,2,1,0:T(8,128)} %slice_add_fusion.2), channel_id=1, source_target_pairs={{0,3},{1,0},{2,1},{3,2},{4,7},{5,4},{6,5},{7,6},{8,11},{9,8},{10,9... | collective-permute-start | bytes 1966088 | tf_op jit(solution)/shard_map/ppermute | solution.py:276
  169.7 30.8 %collective-permute-start.4 = (f32[1,20,64,128]{3,2,1,0:T(8,128)}, f32[1,20,64,128]{3,2,1,0:T(8,128)}, u32[]{:S(2)}, u32[]{:S(2)}) collective-permute-start(f32[1,20,64,128]{3,2,1,0:T(8,128)} %slice_add_fusion.3), channel_id=1, source_target_pairs={{0,1},{1,2},{2,3},{3,0},{4,5},{5,6},{6,7},{7,4},{8,9},{9,10},{10,1... | collective-permute-start | bytes 1966088 | tf_op jit(solution)/shard_map/ppermute | solution.py:275
  183.3 3.0 %copy-start.5 = (f32[1,30,64,128]{3,2,1,0:T(8,128)}, f32[1,30,64,128]{3,2,1,0:T(8,128)S(1)}, u32[]{:S(2)}) copy-start(f32[1,30,64,128]{3,2,1,0:T(8,128)S(1)} %collective-permute-done.8.refs_1_) | copy-start | bytes 2949124
  217.2 2.3 collective-permute-start.9
  220.5 6.3 %collective-permute-start.10 = (f32[128,256]{1,0:T(8,128)S(1)}, f32[128,256]{1,0:T(8,128)S(1)}, u32[]{:S(2)}, u32[]{:S(2)}) collective-permute-start(f32[128,256]{1,0:T(8,128)S(1)} %constant_dynamic-slice_fusion), channel_id=1, source_target_pairs={{0,64},{8,72},{16,80},{24,88},{32,96},{40,104},{48,112},{56,120},{... | collective-permute-start | bytes 393224 | tf_op jit(solution)/shard_map/ppermute | solution.py:224
  226.8 13.7 %collective-permute-start.11 = (f32[128,256]{1,0:T(8,128)S(1)}, f32[128,256]{1,0:T(8,128)S(1)}, u32[]{:S(2)}, u32[]{:S(2)}) collective-permute-start(f32[128,256]{1,0:T(8,128)S(1)} %dynamic-slice_add_fusion.1), channel_id=1, source_target_pairs={{0,16},{8,24},{16,32},{24,40},{32,48},{40,56},{48,0},{56,8},{64,80... | collective-permute-start | bytes 393224 | tf_op jit(solution)/shard_map/ppermute | solution.py:232
  234.2 10.1 %collective-permute-start.12 = (f32[128,256]{1,0:T(8,128)S(1)}, f32[128,256]{1,0:T(8,128)S(1)}, u32[]{:S(2)}, u32[]{:S(2)}) collective-permute-start(f32[128,256]{1,0:T(8,128)S(1)} %dynamic-slice_add_fusion.1), channel_id=1, source_target_pairs={{0,32},{8,40},{16,48},{24,56},{32,0},{40,8},{48,16},{56,24},{64,96... | collective-permute-start | bytes 393224 | tf_op jit(solution)/shard_map/ppermute | solution.py:232
  238.5 5.7 %collective-permute-start.13 = (f32[128,256]{1,0:T(8,128)S(1)}, f32[128,256]{1,0:T(8,128)S(1)}, u32[]{:S(2)}, u32[]{:S(2)}) collective-permute-start(f32[128,256]{1,0:T(8,128)S(1)} %dynamic-slice_add_fusion.1), channel_id=1, source_target_pairs={{0,48},{8,56},{16,0},{24,8},{32,16},{40,24},{48,32},{56,40},{64,11... | collective-permute-start | bytes 393224 | tf_op jit(solution)/shard_map/ppermute | solution.py:232
  244.3 5.4 %collective-permute-start.14 = (f32[128,256]{1,0:T(8,128)S(1)}, f32[128,256]{1,0:T(8,128)S(1)}, u32[]{:S(2)}, u32[]{:S(2)}) collective-permute-start(f32[128,256]{1,0:T(8,128)S(1)} %add_add_fusion), channel_id=1, source_target_pairs={{0,64},{8,72},{16,80},{24,88},{32,96},{40,104},{48,112},{56,120},{... | collective-permute-start | bytes 393224 | tf_op jit(solution)/shard_map/ppermute | solution.py:227
  249.7 4.0 %collective-permute-start.15 = (f32[256,256]{1,0:T(8,128)S(1)}, f32[256,256]{1,0:T(8,128)S(1)}, u32[]{:S(2)}, u32[]{:S(2)}) collective-permute-start(f32[256,256]{1,0:T(8,128)S(1)} %pad_maximum_fusion.3), channel_id=1, source_target_pairs={{0,8},{8,0},{16,24},{24,16},{32,40},{40,32},{48,56},{56,48},{64,72... | collective-permute-start | bytes 786440 | tf_op jit(solution)/shard_map/ppermute | solution.py:227
  254.6 15.2 %copy-start.1 = (f32[512,512]{1,0:T(8,128)S(1)}, f32[512,512]{1,0:T(8,128)}, u32[]{:S(2)}) copy-start(f32[512,512]{1,0:T(8,128)} %param.7) | copy-start | bytes 3145732
  (1 other events, 0.9 us)
